TPU v7x, 512 devices: a whole 4x8x8 slice. The times are simulated.
512 devices in a mesh: grp: 16 (over y, z_lo), dev: 32 (over x, z_hi, core).
Axes of the slice: x: 4, y: 8, z: 8 (z_hi: 4, z_lo: 2; z = z_hi * 2 + z_lo), core: 2. Of those that a mesh axis runs over, the one named last changes fastest.
Arguments:
- points: bfloat16 [1048576, 64], P(('grp', 'dev'))
- inv_scale: float32 [64], replicated, may hold values from 0.15 to 0.45
- probes: float32 [1048576, 32], P(('grp', 'dev'))
- noise: float32 [1], replicated, may hold values from 0.5 to 2
Outputs:
- normalized: float32 [1048576, 32], P(('grp', 'dev'))
- curvature: float32 [32], replicated
All inputs are finite; a program needn't handle non-finite values.
Results may differ from a plain program's by a relative error of at most 0.0065.
Values may be sent and summed in bfloat16 or wider, within the bound.
No kernel may reach another device: no remote copies, remote signals or barrier semaphores. Data moves between devices by JAX's collectives and lax.ppermute only.
A program may use at most 64 MiB of HBM per device.

v0:
```python
import jax
import jax.numpy as jnp
from jax import lax
from jax.sharding import PartitionSpec as P


def from_behind(shard, axis, by):
    count = lax.axis_size(axis)
    return lax.ppermute(shard, axis, [(i, (i + by) % count) for i in range(count)])


def matern(left, left_norm, right, right_norm):
    cross = lax.dot_general(
        left, right, (((1,), (1,)), ((), ())), preferred_element_type=jnp.float32
    )
    dist_sq = jnp.maximum(left_norm[:, None] + right_norm[None, :] - 2.0 * cross, 0.0)
    radius = 5.0**0.5 * jnp.sqrt(dist_sq)
    return ((1.0 + radius + radius * radius / 3.0) * jnp.exp(-radius)).astype(jnp.bfloat16)


def norm_rows(scaled):
    return jnp.sum(jnp.square(scaled.astype(jnp.float32)), axis=1)


def per_device(points, inv_scale, probes, noise):
    scaled = (points.astype(jnp.float32) * inv_scale[None, :]).astype(jnp.bfloat16)
    norms = norm_rows(scaled)
    rounded = probes.astype(jnp.bfloat16)
    self_tile = matern(scaled, norms, scaled, norms)
    local_part = noise[0] * probes + jnp.dot(self_tile, rounded, preferred_element_type=jnp.float32)
    width = lax.axis_size("dev")
    offsets = (1, width, width + 1)
    cross_part = jnp.zeros_like(probes)
    transposed = []
    for offset in offsets:
        far_points, far_probes = from_behind((scaled, rounded), ("grp", "dev"), offset)
        tile = matern(scaled, norms, far_points, norm_rows(far_points))
        cross_part = cross_part + jnp.dot(tile, far_probes, preferred_element_type=jnp.float32)
        transposed.append(
            lax.dot_general(
                tile, rounded, (((0,), (0,)), ((), ())), preferred_element_type=jnp.float32
            )
        )
    wide_probes = rounded.astype(jnp.float32)
    count = lax.axis_size("grp") * lax.axis_size("dev") * probes.shape[0]
    returned = jnp.zeros_like(probes)
    for offset, outgoing in zip(offsets, transposed):
        returned = returned + from_behind(outgoing, ("grp", "dev"), -offset)
    product = local_part + cross_part + returned
    square_local = jnp.sum(product * product, axis=0)
    curv_total, square_total = lax.psum(
        (jnp.sum(wide_probes * product, axis=0), square_local), ("grp", "dev")
    )
    curvature = curv_total / count
    mean_square = square_total / count
    normalized = product * lax.rsqrt(mean_square + 1e-06)[None, :]
    return (normalized, curvature)


def solution(mesh):
    placed = (P(("grp", "dev"), None), P(), P(("grp", "dev"), None), P())
    return jax.shard_map(
        per_device,
        mesh=mesh,
        in_specs=placed,
        out_specs=(P(("grp", "dev"), None), P()),
        check_vma=False,
    )
```

profile of v0, /device:TPU:1, one launch (start us, length us, event | category | flops | bytes accessed | tf_op | source)
XLA Modules:
  0.0 206.5 jit_solution(14169884716192638625)
XLA Ops:
  0.6 1.1 multiply_reduce_fusion.3
  1.8 7.2 %collective-permute-start = (bf16[2048,64]{0,1:T(8,128)(2,1)S(1)}, bf16[2048,64]{0,1:T(8,128)(2,1)S(1)}, u32[]{:S(2)}, u32[]{:S(2)}) collective-permute-start(bf16[2048,64]{0,1:T(8,128)(2,1)S(1)} %get-tuple-element.7), channel_id=1, source_target_pairs={{0,1},{1,2},{2,3},{3,4},{4,5},{5,6},{6,7},{7,8},{8,9},{9,10},{10,1... | collective-permute-start | bytes 786440 | tf_op jit(solution)/shard_map/ppermute | solution.py:9
  9.0 4.0 %collective-permute-start.2 = (bf16[2048,64]{0,1:T(8,128)(2,1)S(1)}, bf16[2048,64]{0,1:T(8,128)(2,1)S(1)}, u32[]{:S(2)}, u32[]{:S(2)}) collective-permute-start(bf16[2048,64]{0,1:T(8,128)(2,1)S(1)} %get-tuple-element.7), channel_id=1, source_target_pairs={{0,32},{1,33},{2,34},{3,35},{4,36},{5,37},{6,38},{7,39},{8,40},{9,... | collective-permute-start | bytes 786440 | tf_op jit(solution)/shard_map/ppermute | solution.py:9
  13.0 2.3 %collective-permute-start.4 = (bf16[2048,64]{0,1:T(8,128)(2,1)S(1)}, bf16[2048,64]{0,1:T(8,128)(2,1)S(1)}, u32[]{:S(2)}, u32[]{:S(2)}) collective-permute-start(bf16[2048,64]{0,1:T(8,128)(2,1)S(1)} %get-tuple-element.7), channel_id=1, source_target_pairs={{0,33},{1,34},{2,35},{3,36},{4,37},{5,38},{6,39},{7,40},{8,41},{9,... | collective-permute-start | bytes 786440 | tf_op jit(solution)/shard_map/ppermute | solution.py:9
  15.3 1.0 convert_element_type.40
  16.3 3.1 %collective-permute-start.3 = (bf16[2048,32]{0,1:T(8,128)(2,1)S(1)}, bf16[2048,32]{0,1:T(8,128)(2,1)S(1)}, u32[]{:S(2)}, u32[]{:S(2)}) collective-permute-start(bf16[2048,32]{0,1:T(8,128)(2,1)S(1)} %convert_element_type.40), channel_id=1, source_target_pairs={{0,32},{1,33},{2,34},{3,35},{4,36},{5,37},{6,38},{7,39},{8,40},{9,... | collective-permute-start | bytes 393224 | tf_op jit(solution)/shard_map/ppermute | solution.py:9
  19.4 8.6 %collective-permute-start.5 = (bf16[2048,32]{0,1:T(8,128)(2,1)S(1)}, bf16[2048,32]{0,1:T(8,128)(2,1)S(1)}, u32[]{:S(2)}, u32[]{:S(2)}) collective-permute-start(bf16[2048,32]{0,1:T(8,128)(2,1)S(1)} %convert_element_type.40), channel_id=1, source_target_pairs={{0,33},{1,34},{2,35},{3,36},{4,37},{5,38},{6,39},{7,40},{8,41},{9,... | collective-permute-start | bytes 393224 | tf_op jit(solution)/shard_map/ppermute | solution.py:9
  28.6 13.1 %fusion.4 = f32[2048,32]{0,1:T(8,128)S(1)} fusion(bf16[2048,32]{0,1:T(8,128)(2,1)S(1)} %convert_element_type.40, bf16[2048,64]{0,1:T(8,128)(2,1)S(1)} %get-tuple-element.7, f32[2048]{0:T(1024)S(1)} %get-tuple-element.6, f32[2048,32]{0,1:T(8,128)} %param.6, f32[]{:T(128)} %bitcast.22), kind=kOutput, calls=%fused_computation.9 | convolution fusion | flops 855769088 | bytes 925700 | tf_op jit(solution)/shard_map/dot_general | solution.py:30
  41.7 0.0 collective-permute-done
  41.7 1.9 collective-permute-start.1
  43.6 0.1 multiply_reduce_fusion.2
  43.7 12.2 %multiply_convert_fusion.2 = bf16[2048,2048]{1,0:T(8,128)(2,1)S(1)} fusion(bf16[2048,64]{0,1:T(8,128)(2,1)S(1)} %get-tuple-element.7, bf16[2048,64]{0,1:T(8,128)(2,1)S(1)} %collective-permute-done, f32[2048]{0:T(1024)S(1)} %multiply_reduce_fusion.2, f32[2048]{0:T(1024)S(1)} %get-tuple-element.6), kind=kOutput, calls=%fused_computation.2 | convolution fusion | flops 587202560 | bytes 8929280 | tf_op jit(solution)/shard_map/dot_general | solution.py:13
  55.9 1.5 fusion.12
  57.4 0.0 collective-permute-done.2
  57.4 2.4 %collective-permute-start.6 = (f32[2048,32]{0,1:T(8,128)S(1)}, f32[2048,32]{0,1:T(8,128)S(1)}, u32[]{:S(2)}, u32[]{:S(2)}) collective-permute-start(f32[2048,32]{0,1:T(8,128)S(1)} %fusion.12), channel_id=1, source_target_pairs={{0,511},{1,0},{2,1},{3,2},{4,3},{5,4},{6,5},{7,6},{8,7},{9,8},{10,... | collective-permute-start | bytes 786440 | tf_op jit(solution)/shard_map/ppermute | solution.py:9
  59.8 0.1 multiply_reduce_fusion.1
  59.9 12.2 %multiply_convert_fusion.1 = bf16[2048,2048]{1,0:T(8,128)(2,1)S(1)} fusion(bf16[2048,64]{0,1:T(8,128)(2,1)S(1)} %get-tuple-element.7, bf16[2048,64]{0,1:T(8,128)(2,1)S(1)} %collective-permute-done.2, f32[2048]{0:T(1024)S(1)} %multiply_reduce_fusion.1, f32[2048]{0:T(1024)S(1)} %get-tuple-element.6), kind=kOutput, calls=%fused_computation.1 | convolution fusion | flops 587202560 | bytes 8929280 | tf_op jit(solution)/shard_map/dot_general | solution.py:13
  72.1 1.5 fusion.13
  73.6 0.0 collective-permute-done.4
  73.7 3.5 %collective-permute-start.7 = (f32[2048,32]{0,1:T(8,128)S(1)}, f32[2048,32]{0,1:T(8,128)S(1)}, u32[]{:S(2)}, u32[]{:S(2)}) collective-permute-start(f32[2048,32]{0,1:T(8,128)S(1)} %fusion.13), channel_id=1, source_target_pairs={{0,480},{1,481},{2,482},{3,483},{4,484},{5,485},{6,486},{7,487},{8... | collective-permute-start | bytes 786440 | tf_op jit(solution)/shard_map/ppermute | solution.py:9
  77.2 0.1 multiply_reduce_fusion
  77.3 12.2 %multiply_convert_fusion = bf16[2048,2048]{1,0:T(8,128)(2,1)S(1)} fusion(bf16[2048,64]{0,1:T(8,128)(2,1)S(1)} %get-tuple-element.7, bf16[2048,64]{0,1:T(8,128)(2,1)S(1)} %collective-permute-done.4, f32[2048]{0:T(1024)S(1)} %multiply_reduce_fusion, f32[2048]{0:T(1024)S(1)} %get-tuple-element.6), kind=kOutput, calls=%fused_computation | convolution fusion | flops 587202560 | bytes 8929280 | tf_op jit(solution)/shard_map/dot_general | solution.py:13
  89.5 1.5 fusion.14
  91.0 0.0 collective-permute-done.3
  91.0 4.1 %collective-permute-start.8 = (f32[2048,32]{0,1:T(8,128)S(1)}, f32[2048,32]{0,1:T(8,128)S(1)}, u32[]{:S(2)}, u32[]{:S(2)}) collective-permute-start(f32[2048,32]{0,1:T(8,128)S(1)} %fusion.14), channel_id=1, source_target_pairs={{0,479},{1,480},{2,481},{3,482},{4,483},{5,484},{6,485},{7,486},{8... | collective-permute-start | bytes 786440 | tf_op jit(solution)/shard_map/ppermute | solution.py:9
  95.1 2.6 %fusion.10 = f32[2048,32]{0,1:T(8,128)S(1)} fusion(bf16[2048,2048]{1,0:T(8,128)(2,1)S(1)} %multiply_convert_fusion.1, bf16[2048,32]{0,1:T(8,128)(2,1)S(1)} %collective-permute-done.3), kind=kOutput, calls=%fused_computation.25 | convolution fusion | flops 268435456 | bytes 8781824 | tf_op jit(solution)/shard_map/dot_general | solution.py:38
  97.7 0.0 collective-permute-done.5
  97.7 2.6 %fusion.11 = f32[2048,32]{0,1:T(8,128)S(1)} fusion(bf16[2048,2048]{1,0:T(8,128)(2,1)S(1)} %multiply_convert_fusion, bf16[2048,32]{0,1:T(8,128)(2,1)S(1)} %collective-permute-done.5), kind=kOutput, calls=%fused_computation.26 | convolution fusion | flops 268435456 | bytes 8781824 | tf_op jit(solution)/shard_map/dot_general | solution.py:38
  100.3 0.0 collective-permute-done.1
  100.3 0.0 collective-permute-done.6
  100.3 0.0 collective-permute-done.7
  100.3 3.8 %collective-permute-done.8 = f32[2048,32]{0,1:T(8,128)S(1)} collective-permute-done((f32[2048,32]{0,1:T(8,128)S(1)}, f32[2048,32]{0,1:T(8,128)S(1)}, u32[]{:S(2)}, u32[]{:S(2)}) %collective-permute-start.8) | collective-permute-done | bytes 262176 | tf_op jit(solution)/shard_map/ppermute | solution.py:9
  104.1 2.7 %multiply_reduce_fusion.4 = (f32[32]{0:T(128)S(1)}, f32[32]{0:T(128)S(1)}, f32[2048,32]{0,1:T(8,128)S(1)}) fusion(bf16[2048,32]{0,1:T(8,128)(2,1)S(1)} %convert_element_type.40, f32[2048,32]{0,1:T(8,128)S(1)} %collective-permute-done.8, f32[2048,32]{0,1:T(8,128)S(1)} %collective-permute-done.6, f32[2048,32]{0,1:T(8,128)S(1)} %collective-permute-done.7, ...), kind=kOutput, calls=%fused_computation.15 | convolution fusion | flops 269156288 | bytes 10486016 | tf_op jit(solution)/shard_map/dot_general | solution.py:38
  106.9 98.3 %all-reduce = (f32[32]{0:T(128)S(1)}, f32[32]{0:T(128)S(1)}) all-reduce(f32[32]{0:T(128)S(1)} %get-tuple-element.3, f32[32]{0:T(128)S(1)} %get-tuple-element.2), channel_id=1, replica_groups=mesh['grp'=16,'dev'=32] {'grp','dev'}, use_global_device_ids=true, to_apply=%region_5.0 | all-reduce | flops 64 | bytes 512 | tf_op jit(solution)/shard_map/psum | solution.py:51
  205.2 0.5 add_rsqrt_fusion
  205.7 0.8 broadcast_multiply_fusion
Async XLA Ops:
  1.8 39.9 %collective-permute-start = (bf16[2048,64]{0,1:T(8,128)(2,1)S(1)}, bf16[2048,64]{0,1:T(8,128)(2,1)S(1)}, u32[]{:S(2)}, u32[]{:S(2)}) collective-permute-start(bf16[2048,64]{0,1:T(8,128)(2,1)S(1)} %get-tuple-element.7), channel_id=1, source_target_pairs={{0,1},{1,2},{2,3},{3,4},{4,5},{5,6},{6,7},{7,8},{8,9},{9,10},{10,1... | collective-permute-start | bytes 786440 | tf_op jit(solution)/shard_map/ppermute | solution.py:9
  9.0 48.5 %collective-permute-start.2 = (bf16[2048,64]{0,1:T(8,128)(2,1)S(1)}, bf16[2048,64]{0,1:T(8,128)(2,1)S(1)}, u32[]{:S(2)}, u32[]{:S(2)}) collective-permute-start(bf16[2048,64]{0,1:T(8,128)(2,1)S(1)} %get-tuple-element.7), channel_id=1, source_target_pairs={{0,32},{1,33},{2,34},{3,35},{4,36},{5,37},{6,38},{7,39},{8,40},{9,... | collective-permute-start | bytes 786440 | tf_op jit(solution)/shard_map/ppermute | solution.py:9
  13.0 60.7 %collective-permute-start.4 = (bf16[2048,64]{0,1:T(8,128)(2,1)S(1)}, bf16[2048,64]{0,1:T(8,128)(2,1)S(1)}, u32[]{:S(2)}, u32[]{:S(2)}) collective-permute-start(bf16[2048,64]{0,1:T(8,128)(2,1)S(1)} %get-tuple-element.7), channel_id=1, source_target_pairs={{0,33},{1,34},{2,35},{3,36},{4,37},{5,38},{6,39},{7,40},{8,41},{9,... | collective-permute-start | bytes 786440 | tf_op jit(solution)/shard_map/ppermute | solution.py:9
  16.3 74.7 %collective-permute-start.3 = (bf16[2048,32]{0,1:T(8,128)(2,1)S(1)}, bf16[2048,32]{0,1:T(8,128)(2,1)S(1)}, u32[]{:S(2)}, u32[]{:S(2)}) collective-permute-start(bf16[2048,32]{0,1:T(8,128)(2,1)S(1)} %convert_element_type.40), channel_id=1, source_target_pairs={{0,32},{1,33},{2,34},{3,35},{4,36},{5,37},{6,38},{7,39},{8,40},{9,... | collective-permute-start | bytes 393224 | tf_op jit(solution)/shard_map/ppermute | solution.py:9
  19.4 78.3 %collective-permute-start.5 = (bf16[2048,32]{0,1:T(8,128)(2,1)S(1)}, bf16[2048,32]{0,1:T(8,128)(2,1)S(1)}, u32[]{:S(2)}, u32[]{:S(2)}) collective-permute-start(bf16[2048,32]{0,1:T(8,128)(2,1)S(1)} %convert_element_type.40), channel_id=1, source_target_pairs={{0,33},{1,34},{2,35},{3,36},{4,37},{5,38},{6,39},{7,40},{8,41},{9,... | collective-permute-start | bytes 393224 | tf_op jit(solution)/shard_map/ppermute | solution.py:9
  41.7 58.6 %collective-permute-start.1 = (bf16[2048,32]{0,1:T(8,128)(2,1)S(1)}, bf16[2048,32]{0,1:T(8,128)(2,1)S(1)}, u32[]{:S(2)}, u32[]{:S(2)}) collective-permute-start(bf16[2048,32]{0,1:T(8,128)(2,1)S(1)} %convert_element_type.40), channel_id=1, source_target_pairs={{0,1},{1,2},{2,3},{3,4},{4,5},{5,6},{6,7},{7,8},{8,9},{9,10},{10,1... | collective-permute-start | bytes 393224 | tf_op jit(solution)/shard_map/ppermute | solution.py:9
  57.4 42.9 %collective-permute-start.6 = (f32[2048,32]{0,1:T(8,128)S(1)}, f32[2048,32]{0,1:T(8,128)S(1)}, u32[]{:S(2)}, u32[]{:S(2)}) collective-permute-start(f32[2048,32]{0,1:T(8,128)S(1)} %fusion.12), channel_id=1, source_target_pairs={{0,511},{1,0},{2,1},{3,2},{4,3},{5,4},{6,5},{7,6},{8,7},{9,8},{10,... | collective-permute-start | bytes 786440 | tf_op jit(solution)/shard_map/ppermute | solution.py:9
  73.7 26.7 %collective-permute-start.7 = (f32[2048,32]{0,1:T(8,128)S(1)}, f32[2048,32]{0,1:T(8,128)S(1)}, u32[]{:S(2)}, u32[]{:S(2)}) collective-permute-start(f32[2048,32]{0,1:T(8,128)S(1)} %fusion.13), channel_id=1, source_target_pairs={{0,480},{1,481},{2,482},{3,483},{4,484},{5,485},{6,486},{7,487},{8... | collective-permute-start | bytes 786440 | tf_op jit(solution)/shard_map/ppermute | solution.py:9
  91.0 13.1 %collective-permute-start.8 = (f32[2048,32]{0,1:T(8,128)S(1)}, f32[2048,32]{0,1:T(8,128)S(1)}, u32[]{:S(2)}, u32[]{:S(2)}) collective-permute-start(f32[2048,32]{0,1:T(8,128)S(1)} %fusion.14), channel_id=1, source_target_pairs={{0,479},{1,480},{2,481},{3,482},{4,483},{5,484},{6,485},{7,486},{8... | collective-permute-start | bytes 786440 | tf_op jit(solution)/shard_map/ppermute | solution.py:9
where the time goes:
time: 207 us
  blocking collectives  98.3 us (47%)
  matrix products  62.2 us (30%)
  starting transfers between devices  37.1 us (18%)
  waiting for transfers between devices  3.84 us (2%)
  other arithmetic  3.61 us (2%)
    psum x1, blocking collectives, per_device(): lax.psum((jnp.sum(wide_probes * product, axis=0), square_local), ('grp',...  98.3 us
    ppermute x9, starting transfers between devices, from_behind(): lax.ppermute(shard, axis, [(i, (i + by) % count) for i in range(count)])  37.1 us
    dot_general x3, matrix products, matern(): lax.dot_general(left, right, (((1,), (1,)), ((), ())), preferred_element_...  36.6 us
    dot_general x1, matrix products, per_device(): jnp.dot(self_tile, rounded, preferred_element_type=jnp.float32)  13.1 us
    dot_general x3, matrix products, per_device(): jnp.dot(tile, far_probes, preferred_element_type=jnp.float32)  7.91 us
    dot_general x3, matrix products, per_device(): lax.dot_general(tile, rounded, (((0,), (0,)), ((), ())), preferred_elemen...  4.62 us
  transfers between devices with their start and end apart: 9, of which 1 were waited for; matrix products, arithmetic and copies ran while one was open for 29% of the time, Pallas kernels for 0%

commit v1 on v0

v1 whole, which is shorter than its diff:
```python
import functools

import jax
import jax.numpy as jnp
from jax import lax
from jax.experimental import pallas as pl
from jax.experimental.pallas import tpu as pltpu
from jax.sharding import PartitionSpec as P

ROOT5 = 5.0**0.5
RATE = ROOT5 * 1.4426950408889634
DEPTH = 128
VMEM = pl.BlockSpec(memory_space=pltpu.VMEM)


def dot(left, right, dims):
    return lax.dot_general(left, right, (dims, ((), ())), preferred_element_type=jnp.float32)


def matern(dist_sq):
    dist_sq = jnp.maximum(dist_sq, 1e-30)
    dist = dist_sq * lax.rsqrt(dist_sq)
    decay = jnp.exp2(dist * -RATE)
    moved = dist + 1.5 / ROOT5
    return ((moved * moved + 0.15) * decay).astype(jnp.bfloat16)


def extended(features, left):
    wide = features.astype(jnp.float32)
    norms = jnp.sum(wide * wide, axis=0, keepdims=True)
    high = norms.astype(jnp.bfloat16).astype(jnp.float32)
    rest = norms - high
    mid = rest.astype(jnp.bfloat16).astype(jnp.float32)
    low = rest - mid
    first, ones = (3, 0) if left else (0, 3)
    row = lax.broadcasted_iota(jnp.int32, (DEPTH - features.shape[0], features.shape[1]), 0)
    extra = jnp.where((row >= ones) & (row < ones + 3), 1.0, 0.0)
    for k, part in enumerate((high, mid, low)):
        extra = jnp.where(row == first + k, part, extra)
    wide = wide * -2.0 if left else wide
    return jnp.concatenate([wide, extra], axis=0).astype(jnp.bfloat16)


def put_left(left_ref, features):
    left_ref[...] = extended(features, True).astype(jnp.float32).T.astype(jnp.bfloat16)


def fill(tile_ref, dist_ref):
    for row in range(0, dist_ref.shape[0], 32):
        tile_ref[row : row + 32, :] = matern(dist_ref[row : row + 32, :])


def pair_kernel(rows, cols, feats, own_ref, far_ref, out_ref, back_ref, left, right, dist0, dist1, tile0, tile1, back):
    count = own_ref.shape[1]
    per, steps = count // rows, (count // rows) * (count // cols)
    right[...] = extended(own_ref[:feats, :], False)
    put_left(left, far_ref[:feats, :])
    out_ref[...] = jnp.zeros_like(out_ref)
    back[...] = jnp.zeros_like(back)

    def spans(step):
        return (
            pl.ds(pl.multiple_of(lax.rem(step, per) * rows, rows), rows),
            pl.ds(pl.multiple_of(lax.div(step, per) * cols, cols), cols),
        )

    def measure(step, dist):
        far, own = spans(step)
        dist[...] = dot(left[far, :], right[:, own], ((1,), (0,)))

    def apply(step, tile):
        far, own = spans(step)
        out_ref[:, own] += dot(far_ref[feats:, far], tile[...], ((1,), (0,)))
        back[:, far] += dot(own_ref[feats:, own], tile[...], ((1,), (1,)))

    measure(jnp.int32(0), dist0)
    measure(jnp.int32(1), dist1)
    fill(tile0, dist0)

    def body(half, carry):
        step = 2 * half
        apply(step - 2, tile0)
        fill(tile1, dist1)
        measure(step, dist0)
        apply(step - 1, tile1)
        fill(tile0, dist0)
        measure(step + 1, dist1)
        return carry

    lax.fori_loop(1, steps // 2, body, 0)
    apply(jnp.int32(steps - 2), tile0)
    fill(tile1, dist1)
    apply(jnp.int32(steps - 1), tile1)
    back_ref[...] = back[...].astype(back_ref.dtype)


def pair(own, far, feats, rows=512, cols=256):
    count = own.shape[1]
    probes = own.shape[0] - feats
    return pl.pallas_call(
        functools.partial(pair_kernel, rows, cols, feats),
        out_shape=(
            jax.ShapeDtypeStruct((probes, count), jnp.float32),
            jax.ShapeDtypeStruct((probes, count), jnp.bfloat16),
        ),
        in_specs=[VMEM] * 2,
        out_specs=[VMEM] * 2,
        scratch_shapes=[
            pltpu.VMEM((count, DEPTH), jnp.bfloat16),
            pltpu.VMEM((DEPTH, count), jnp.bfloat16),
            pltpu.VMEM((rows, cols), jnp.float32),
            pltpu.VMEM((rows, cols), jnp.float32),
            pltpu.VMEM((rows, cols), jnp.bfloat16),
            pltpu.VMEM((rows, cols), jnp.bfloat16),
            pltpu.VMEM((probes, count), jnp.float32),
        ],
        compiler_params=pltpu.CompilerParams(vmem_limit_bytes=32 * 2**20),
        cost_estimate=pl.CostEstimate(
            flops=2 * count * count * (2 * 256 + DEPTH),
            bytes_accessed=count * 1000,
            transcendentals=2 * count * count,
        ),
    )(own, far)


def self_kernel(cols, feats, own_ref, out_ref, left, right, dist0, dist1, tile0, tile1):
    count = own_ref.shape[1]
    blocks = count // cols
    half = blocks // 2
    right[...] = extended(own_ref[:feats, :], False)
    put_left(left, own_ref[:feats, :])
    out_ref[...] = jnp.zeros_like(out_ref)

    def span(block):
        return pl.ds(pl.multiple_of(lax.rem(block, blocks) * cols, cols), cols)

    def measure(i, pieces, dist):
        for k, d in enumerate(pieces):
            dist[k * cols : (k + 1) * cols, :] = dot(left[span(i + d), :], right[:, span(i)], ((1,), (0,)))

    def apply(i, pieces, tile, both):
        total = jnp.zeros((out_ref.shape[0], cols), jnp.float32)
        for k, d in enumerate(pieces):
            part = tile[k * cols : (k + 1) * cols, :]
            total += dot(own_ref[feats:, span(i + d)], part, ((1,), (0,)))
            if both:
                out_ref[:, span(i + d)] += dot(own_ref[feats:, span(i)], part, ((1,), (1,)))
        out_ref[:, span(i)] += total

    once, twice = (0, half), tuple(range(1, half))
    measure(jnp.int32(0), once, dist0)
    measure(jnp.int32(0), twice, dist1)
    fill(tile0, dist0)

    def body(i, carry):
        apply(i - 1, once, tile0, False)
        fill(tile1, dist1)
        measure(i, once, dist0)
        apply(i - 1, twice, tile1, True)
        fill(tile0, dist0)
        measure(i, twice, dist1)
        return carry

    lax.fori_loop(1, blocks, body, 0)
    apply(jnp.int32(blocks - 1), once, tile0, False)
    fill(tile1, dist1)
    apply(jnp.int32(blocks - 1), twice, tile1, True)


def self_product(own, feats, cols=256):
    count = own.shape[1]
    probes = own.shape[0] - feats
    twice = (count // cols // 2 - 1) * cols
    return pl.pallas_call(
        functools.partial(self_kernel, cols, feats),
        out_shape=jax.ShapeDtypeStruct((probes, count), jnp.float32),
        in_specs=[VMEM],
        out_specs=VMEM,
        scratch_shapes=[
            pltpu.VMEM((count, DEPTH), jnp.bfloat16),
            pltpu.VMEM((DEPTH, count), jnp.bfloat16),
            pltpu.VMEM((2 * cols, cols), jnp.float32),
            pltpu.VMEM((twice, cols), jnp.float32),
            pltpu.VMEM((2 * cols, cols), jnp.bfloat16),
            pltpu.VMEM((twice, cols), jnp.bfloat16),
        ],
        compiler_params=pltpu.CompilerParams(vmem_limit_bytes=32 * 2**20),
        cost_estimate=pl.CostEstimate(
            flops=count * count * (3 * 256 + DEPTH),
            bytes_accessed=count * 500,
            transcendentals=count * count,
        ),
    )(own)


def from_behind(shard, by):
    count = lax.axis_size("grp") * lax.axis_size("dev")
    return lax.ppermute(shard, ("grp", "dev"), [(i, (i + by) % count) for i in range(count)])


def total(partial):
    for axis in ("dev", "grp"):
        size = lax.axis_size(axis)
        copies = jnp.broadcast_to(partial[None, :], (size, partial.shape[0]))
        partial = jnp.sum(lax.all_to_all(copies, axis, 0, 0), axis=0)
    return partial


def per_device(points, inv_scale, probes, noise):
    feats = points.shape[1]
    wide = probes.T
    scaled = (points.T.astype(jnp.float32) * inv_scale[:, None]).astype(jnp.bfloat16)
    rounded = wide.astype(jnp.bfloat16)
    own = jnp.concatenate([scaled, rounded], axis=0)
    width = lax.axis_size("dev")
    offsets = (1, width, width + 1)
    far = [from_behind(own, offset) for offset in offsets]
    parts = [self_product(own, feats)]
    for offset, other in zip(offsets, far):
        out, back = pair(own, other, feats)
        parts.append(out)
        parts.append(from_behind(back, -offset).astype(jnp.float32))
    product = noise[0] * wide + sum(parts) * (5.0 / 3.0)
    count = lax.axis_size("grp") * width * probes.shape[0]
    sums = total(
        jnp.concatenate([jnp.sum(rounded.astype(jnp.float32) * product, axis=1), jnp.sum(product * product, axis=1)])
    )
    mean = sums / count
    curvature, mean_square = jnp.split(mean, 2)
    normalized = product * lax.rsqrt(mean_square + 1e-06)[:, None]
    return (normalized.T, curvature)


def solution(mesh):
    placed = (P(("grp", "dev"), None), P(), P(("grp", "dev"), None), P())
    return jax.shard_map(
        per_device,
        mesh=mesh,
        in_specs=placed,
        out_specs=(P(("grp", "dev"), None), P()),
        check_vma=False,
    )
```

time: 207 us -> 103 us (0.50)
  blocking collectives: 98.3 us -> 27.5 us
  matrix products: 62.2 us -> 0 us
  Pallas kernels: 0 us -> 30.8 us
  waiting for transfers between devices: 3.84 us -> 0.02 us
  starting transfers between devices: 37.1 us -> 40 us
    psum x1 -> x0, blocking collectives: 98.3 us -> none  [per_device(): lax.psum((jnp.sum(wide_probes * product, axis=0), square_local), ('grp',...]
    dot_general x10 -> x0, matrix products: 62.2 us -> none  [the longest x3 36.6 us: matern(): lax.dot_general(left, right, (((1,), (1,)), ((), ())), preferred_element_...]
    pallas_call x0 -> x4, Pallas kernels: none -> 30.8 us  [the longest x3 25.2 us: pair(): pl.pallas_call(functools.partial(pair_kernel, rows, cols, feats), out_sha...]
    all_to_all x0 -> x2, blocking collectives: none -> 27.5 us  [total(): partial = jnp.sum(lax.all_to_all(copies, axis, 0, 0), axis=0)]
    ppermute x9 -> x6, waiting for transfers between devices: 3.84 us -> 0.02 us  [from_behind(): lax.ppermute(shard, ('grp', 'dev'), [(i, (i + by) % count) for i in range...]
    ppermute x9 -> x6, starting transfers between devices: 37.1 us -> 40 us  [from_behind(): lax.ppermute(shard, ('grp', 'dev'), [(i, (i + by) % count) for i in range...]
  transfers between devices with their start and end apart: 9 -> 6, of which waited for: 1 -> 0; matrix products, arithmetic and copies ran while one was open for 29% -> 0% of each run, Pallas kernels for 0% -> 30%
where the time goes in v1:
time: 103 us
  starting transfers between devices  40 us (39%)
  Pallas kernels  30.8 us (30%)
  blocking collectives  27.5 us (27%)
  other arithmetic  2.83 us (3%)
  between operations  1.47 us (1%)
    ppermute x6, starting transfers between devices, from_behind(): lax.ppermute(shard, ('grp', 'dev'), [(i, (i + by) % count) for i in range...  40 us
    all_to_all x2, blocking collectives, total(): partial = jnp.sum(lax.all_to_all(copies, axis, 0, 0), axis=0)  27.5 us
    pallas_call x3, Pallas kernels, pair(): pl.pallas_call(functools.partial(pair_kernel, rows, cols, feats), out_sha...  25.2 us
    pallas_call x1, Pallas kernels, self_product(): pl.pallas_call(functools.partial(self_kernel, cols, feats), out_shape=jax...  5.61 us
  transfers between devices with their start and end apart: 6, of which 0 were waited for; matrix products, arithmetic and copies ran while one was open for 0% of the time, Pallas kernels for 30%

profile of v1, /device:TPU:1, one launch (start us, length us, event | category | flops | bytes accessed | tf_op | source)
XLA Modules:
  0.0 102.7 jit_solution(3143791455693475562)
XLA Ops:
  0.6 0.0 copy-start.1
  0.6 0.0 copy-start.2
  0.6 1.0 convert_bitcast_fusion
  1.7 0.0 copy-done.1
  1.7 0.0 copy-done.2
  1.7 0.1 fusion
  1.8 7.2 %collective-permute-start = (bf16[96,2048]{1,0:T(8,128)(2,1)S(1)}, bf16[96,2048]{1,0:T(8,128)(2,1)S(1)}, u32[]{:S(2)}, u32[]{:S(2)}) collective-permute-start(bf16[96,2048]{1,0:T(8,128)(2,1)S(1)} %pad_maximum_fusion.own_ref), channel_id=1, source_target_pairs={{0,1},{1,2},{2,3},{3,4},{4,5},{5,6},{6,7},{7,8},{8,9},{9,10},{10,1... | collective-permute-start | bytes 1179656 | tf_op jit(solution)/shard_map/ppermute | solution.py:198
  9.0 4.0 %collective-permute-start.2 = (bf16[96,2048]{1,0:T(8,128)(2,1)S(1)}, bf16[96,2048]{1,0:T(8,128)(2,1)S(1)}, u32[]{:S(2)}, u32[]{:S(2)}) collective-permute-start(bf16[96,2048]{1,0:T(8,128)(2,1)S(1)} %pad_maximum_fusion.own_ref), channel_id=1, source_target_pairs={{0,32},{1,33},{2,34},{3,35},{4,36},{5,37},{6,38},{7,39},{8,40},{9,... | collective-permute-start | bytes 1179656 | tf_op jit(solution)/shard_map/ppermute | solution.py:198
  13.0 2.3 %collective-permute-start.4 = (bf16[96,2048]{1,0:T(8,128)(2,1)S(1)}, bf16[96,2048]{1,0:T(8,128)(2,1)S(1)}, u32[]{:S(2)}, u32[]{:S(2)}) collective-permute-start(bf16[96,2048]{1,0:T(8,128)(2,1)S(1)} %pad_maximum_fusion.own_ref), channel_id=1, source_target_pairs={{0,33},{1,34},{2,35},{3,36},{4,37},{5,38},{6,39},{7,40},{8,41},{9,... | collective-permute-start | bytes 1179656 | tf_op jit(solution)/shard_map/ppermute | solution.py:198
  15.4 0.0 collective-permute-done.far_ref
  15.4 8.4 %shard_map.60 = (f32[32,2048]{1,0:T(8,128)S(1)}, bf16[32,2048]{1,0:T(8,128)(2,1)S(1)}) custom-call(bf16[96,2048]{1,0:T(8,128)(2,1)S(1)} %pad_maximum_fusion.own_ref, bf16[96,2048]{1,0:T(8,128)(2,1)S(1)} %collective-permute-done.far_ref), custom_call_target="tpu_custom_call" | custom-call | flops 5368709120 | bytes 2048000 | tf_op jit(solution)/shard_map/pallas_call | solution.py:100
  23.8 13.1 %collective-permute-start.1 = (bf16[32,2048]{1,0:T(8,128)(2,1)S(1)}, bf16[32,2048]{1,0:T(8,128)(2,1)S(1)}, u32[]{:S(2)}, u32[]{:S(2)}) collective-permute-start(bf16[32,2048]{1,0:T(8,128)(2,1)S(1)} %get-tuple-element.9), channel_id=1, source_target_pairs={{0,511},{1,0},{2,1},{3,2},{4,3},{5,4},{6,5},{7,6},{8,7},{9,8},{10,... | collective-permute-start | bytes 393224 | tf_op jit(solution)/shard_map/ppermute | solution.py:198
  36.9 0.0 collective-permute-done.2.far_ref
  36.9 8.4 %shard_map.61 = (f32[32,2048]{1,0:T(8,128)S(1)}, bf16[32,2048]{1,0:T(8,128)(2,1)S(1)}) custom-call(bf16[96,2048]{1,0:T(8,128)(2,1)S(1)} %pad_maximum_fusion.own_ref, bf16[96,2048]{1,0:T(8,128)(2,1)S(1)} %collective-permute-done.2.far_ref), custom_call_target="tpu_custom_call" | custom-call | flops 5368709120 | bytes 2048000 | tf_op jit(solution)/shard_map/pallas_call | solution.py:100
  45.3 11.3 %collective-permute-start.3 = (bf16[32,2048]{1,0:T(8,128)(2,1)S(1)}, bf16[32,2048]{1,0:T(8,128)(2,1)S(1)}, u32[]{:S(2)}, u32[]{:S(2)}) collective-permute-start(bf16[32,2048]{1,0:T(8,128)(2,1)S(1)} %get-tuple-element.11), channel_id=1, source_target_pairs={{0,480},{1,481},{2,482},{3,483},{4,484},{5,485},{6,486},{7,487},{8... | collective-permute-start | bytes 393224 | tf_op jit(solution)/shard_map/ppermute | solution.py:198
  56.7 0.0 collective-permute-done.4.far_ref
  56.7 8.4 %shard_map.62 = (f32[32,2048]{1,0:T(8,128)S(1)}, bf16[32,2048]{1,0:T(8,128)(2,1)S(1)}) custom-call(bf16[96,2048]{1,0:T(8,128)(2,1)S(1)} %pad_maximum_fusion.own_ref, bf16[96,2048]{1,0:T(8,128)(2,1)S(1)} %collective-permute-done.4.far_ref), custom_call_target="tpu_custom_call" | custom-call | flops 5368709120 | bytes 2048000 | tf_op jit(solution)/shard_map/pallas_call | solution.py:100
  65.1 0.0 copy-start
  65.1 2.1 %collective-permute-start.5 = (bf16[32,2048]{1,0:T(8,128)(2,1)S(1)}, bf16[32,2048]{1,0:T(8,128)(2,1)S(1)}, u32[]{:S(2)}, u32[]{:S(2)}) collective-permute-start(bf16[32,2048]{1,0:T(8,128)(2,1)S(1)} %get-tuple-element.13), channel_id=1, source_target_pairs={{0,479},{1,480},{2,481},{3,482},{4,483},{5,484},{6,485},{7,486},{8... | collective-permute-start | bytes 393224 | tf_op jit(solution)/shard_map/ppermute | solution.py:198
  67.2 5.6 %shard_map.59 = f32[32,2048]{1,0:T(8,128)S(1)} custom-call(bf16[96,2048]{1,0:T(8,128)(2,1)S(1)} %pad_maximum_fusion.own_ref), custom_call_target="tpu_custom_call" | custom-call | flops 3758096384 | bytes 1024000 | tf_op jit(solution)/shard_map/pallas_call | solution.py:174
  73.4 0.0 collective-permute-done.1
  73.4 0.0 collective-permute-done.3
  73.4 0.0 collective-permute-done.5
  73.5 0.0 copy-done
  73.5 0.3 multiply_reduce_fusion.1
  73.7 0.1 pad_maximum_fusion.1
  73.8 13.0 %all_to_all.12 = f32[32,1,64]{2,1,0:T(1,128)S(1)} all-to-all(f32[32,1,64]{2,1,0:T(1,128)S(1)} %broadcast_in_dim.4), channel_id=1, replica_groups=mesh['grp'=16,'dev'=32] {'dev'}, dimensions={0} | all-to-all | bytes 16384 | tf_op jit(solution)/shard_map/all_to_all | solution.py:205
  86.8 14.5 %all_to_all.13 = f32[16,1,64]{2,1,0:T(1,128)S(1)} all-to-all(f32[16,1,64]{2,1,0:T(1,128)S(1)} %broadcast_in_dim.5), channel_id=1, replica_groups=mesh['grp'=16,'dev'=32] {'grp'}, dimensions={0} | all-to-all | bytes 8192 | tf_op jit(solution)/shard_map/all_to_all | solution.py:205
  101.4 0.5 fusion.1
  101.9 0.8 multiply_bitcast_fusion
  (6 shorter events, 0.1 us)
Async XLA Ops:
  0.6 1.0 %copy-start.1 = (bf16[2048,64]{0,1:T(8,128)(2,1)S(1)}, bf16[2048,64]{0,1:T(8,128)(2,1)}, u32[]{:S(2)}) copy-start(bf16[2048,64]{0,1:T(8,128)(2,1)} %param.4) | copy-start | bytes 786436
  0.6 1.0 %copy-start.2 = (f32[64]{0:T(128)S(1)}, f32[64]{0:T(128)}, u32[]{:S(2)}) copy-start(f32[64]{0:T(128)} %param.5) | copy-start | bytes 772
  1.8 13.5 %collective-permute-start = (bf16[96,2048]{1,0:T(8,128)(2,1)S(1)}, bf16[96,2048]{1,0:T(8,128)(2,1)S(1)}, u32[]{:S(2)}, u32[]{:S(2)}) collective-permute-start(bf16[96,2048]{1,0:T(8,128)(2,1)S(1)} %pad_maximum_fusion.own_ref), channel_id=1, source_target_pairs={{0,1},{1,2},{2,3},{3,4},{4,5},{5,6},{6,7},{7,8},{8,9},{9,10},{10,1... | collective-permute-start | bytes 1179656 | tf_op jit(solution)/shard_map/ppermute | solution.py:198
  9.0 27.9 %collective-permute-start.2 = (bf16[96,2048]{1,0:T(8,128)(2,1)S(1)}, bf16[96,2048]{1,0:T(8,128)(2,1)S(1)}, u32[]{:S(2)}, u32[]{:S(2)}) collective-permute-start(bf16[96,2048]{1,0:T(8,128)(2,1)S(1)} %pad_maximum_fusion.own_ref), channel_id=1, source_target_pairs={{0,32},{1,33},{2,34},{3,35},{4,36},{5,37},{6,38},{7,39},{8,40},{9,... | collective-permute-start | bytes 1179656 | tf_op jit(solution)/shard_map/ppermute | solution.py:198
  13.0 43.6 %collective-permute-start.4 = (bf16[96,2048]{1,0:T(8,128)(2,1)S(1)}, bf16[96,2048]{1,0:T(8,128)(2,1)S(1)}, u32[]{:S(2)}, u32[]{:S(2)}) collective-permute-start(bf16[96,2048]{1,0:T(8,128)(2,1)S(1)} %pad_maximum_fusion.own_ref), channel_id=1, source_target_pairs={{0,33},{1,34},{2,35},{3,36},{4,37},{5,38},{6,39},{7,40},{8,41},{9,... | collective-permute-start | bytes 1179656 | tf_op jit(solution)/shard_map/ppermute | solution.py:198
  23.8 49.7 %collective-permute-start.1 = (bf16[32,2048]{1,0:T(8,128)(2,1)S(1)}, bf16[32,2048]{1,0:T(8,128)(2,1)S(1)}, u32[]{:S(2)}, u32[]{:S(2)}) collective-permute-start(bf16[32,2048]{1,0:T(8,128)(2,1)S(1)} %get-tuple-element.9), channel_id=1, source_target_pairs={{0,511},{1,0},{2,1},{3,2},{4,3},{5,4},{6,5},{7,6},{8,7},{9,8},{10,... | collective-permute-start | bytes 393224 | tf_op jit(solution)/shard_map/ppermute | solution.py:198
  45.3 28.1 %collective-permute-start.3 = (bf16[32,2048]{1,0:T(8,128)(2,1)S(1)}, bf16[32,2048]{1,0:T(8,128)(2,1)S(1)}, u32[]{:S(2)}, u32[]{:S(2)}) collective-permute-start(bf16[32,2048]{1,0:T(8,128)(2,1)S(1)} %get-tuple-element.11), channel_id=1, source_target_pairs={{0,480},{1,481},{2,482},{3,483},{4,484},{5,485},{6,486},{7,487},{8... | collective-permute-start | bytes 393224 | tf_op jit(solution)/shard_map/ppermute | solution.py:198
  65.1 8.4 %copy-start = (f32[2048,32]{0,1:T(8,128)S(1)}, f32[2048,32]{0,1:T(8,128)}, u32[]{:S(2)}) copy-start(f32[2048,32]{0,1:T(8,128)} %param.6) | copy-start | bytes 786436
  65.1 8.4 %collective-permute-start.5 = (bf16[32,2048]{1,0:T(8,128)(2,1)S(1)}, bf16[32,2048]{1,0:T(8,128)(2,1)S(1)}, u32[]{:S(2)}, u32[]{:S(2)}) collective-permute-start(bf16[32,2048]{1,0:T(8,128)(2,1)S(1)} %get-tuple-element.13), channel_id=1, source_target_pairs={{0,479},{1,480},{2,481},{3,482},{4,483},{5,484},{6,485},{7,486},{8... | collective-permute-start | bytes 393224 | tf_op jit(solution)/shard_map/ppermute | solution.py:198

commit v2 on v0

v2 whole, which is shorter than its diff:
```python
import functools

import jax
import jax.numpy as jnp
from jax import lax
from jax.experimental import pallas as pl
from jax.experimental.pallas import tpu as pltpu
from jax.sharding import PartitionSpec as P

LOG2E = 1.4426950408889634
DEPTH = 256
EXTRA = 16
COLS = 256
ROWS = 512
VMEM = pl.BlockSpec(memory_space=pltpu.VMEM)
PARAMS = pltpu.CompilerParams(vmem_limit_bytes=32 * 2**20)


def dot(left, right, dims):
    return lax.dot_general(left, right, (dims, ((), ())), preferred_element_type=jnp.float32)


def matern(third_sq):
    third_sq = jnp.maximum(third_sq, 1e-30)
    third = third_sq * lax.rsqrt(third_sq)
    decay = jnp.exp2(third * (-3.0 * LOG2E))
    return ((third_sq + third + 1.0 / 3.0) * decay).astype(jnp.bfloat16)


def split3(wide):
    high = wide.astype(jnp.bfloat16)
    rest = wide - high.astype(jnp.float32)
    mid = rest.astype(jnp.bfloat16)
    low = (rest - mid.astype(jnp.float32)).astype(jnp.bfloat16)
    return high, mid, low


def extra_rows(features, left):
    wide = features.astype(jnp.float32)
    parts = split3(jnp.sum(wide * wide, axis=0, keepdims=True) * (5.0 / 9.0))
    row = lax.broadcasted_iota(jnp.int32, (EXTRA, features.shape[1]), 0)
    first, ones = (3, 0) if left else (0, 3)
    extra = jnp.where((row >= ones) & (row < ones + 3), 1.0, 0.0)
    for k, part in enumerate(parts):
        extra = jnp.where(row == first + k, part.astype(jnp.float32), extra)
    return extra.astype(jnp.bfloat16)


def left_side(features):
    feats, count = features.shape
    parts = split3(features.astype(jnp.float32) * (-10.0 / 9.0))
    rest = jnp.zeros((DEPTH - 3 * feats - EXTRA, count), jnp.bfloat16)
    return jnp.concatenate([*parts, extra_rows(features, True), rest], axis=0).T


def put_right(right, features):
    feats, count = features.shape
    for k in range(3):
        right[k * feats : (k + 1) * feats, :] = features
    right[3 * feats : 3 * feats + EXTRA, :] = extra_rows(features, False)
    right[3 * feats + EXTRA :, :] = jnp.zeros((DEPTH - 3 * feats - EXTRA, count), jnp.bfloat16)


def run_steps(steps, measure, apply, dists, tiles):
    def fill(step, slot):
        for row in range(0, step[1], 32):
            tiles[slot][row : row + 32, :] = matern(dists[slot][row : row + 32, :])

    count = len(steps)
    for k in range(count + 2):
        if k >= 2:
            apply(steps[k - 2], tiles[k % 2])
        if 1 <= k <= count:
            fill(steps[k - 1], (k - 1) % 2)
        if k < count:
            measure(steps[k], dists[k % 2])


def pair_kernel(feats, left_ref, own_ref, far_ref, acc_ref, out_ref, back_ref, right, dist0, dist1, tile0, tile1, back):
    count = own_ref.shape[1]
    put_right(right, far_ref[:feats, :])
    out_ref[...] = acc_ref[...]
    back[...] = jnp.zeros_like(back)

    def measure(step, dist):
        row, rows, col = step
        dist[...] = dot(left_ref[row : row + rows, :], right[:, col : col + COLS], ((1,), (0,)))

    def apply(step, tile):
        row, rows, col = step
        out_ref[:, row : row + rows] += dot(far_ref[feats:, col : col + COLS], tile[...], ((1,), (1,)))
        back[:, col : col + COLS] += dot(own_ref[feats:, row : row + rows], tile[...], ((1,), (0,)))

    steps = [(row, ROWS, col) for col in range(0, count, COLS) for row in range(0, count, ROWS)]
    run_steps(steps, measure, apply, (dist0, dist1), (tile0, tile1))
    back_ref[...] = back[...].astype(back_ref.dtype)


def stage_buffers():
    return [
        pltpu.VMEM((ROWS, COLS), jnp.float32),
        pltpu.VMEM((ROWS, COLS), jnp.float32),
        pltpu.VMEM((ROWS, COLS), jnp.bfloat16),
        pltpu.VMEM((ROWS, COLS), jnp.bfloat16),
    ]


def cost(elements):
    return pl.CostEstimate(flops=elements * 1500, bytes_accessed=2**20, transcendentals=2 * elements)


def pair(left, own, far, acc, feats):
    probes, count = acc.shape
    return pl.pallas_call(
        functools.partial(pair_kernel, feats),
        out_shape=(
            jax.ShapeDtypeStruct((probes, count), jnp.float32),
            jax.ShapeDtypeStruct((probes, count), jnp.bfloat16),
        ),
        in_specs=[VMEM] * 4,
        out_specs=[VMEM] * 2,
        scratch_shapes=[
            pltpu.VMEM((DEPTH, count), jnp.bfloat16),
            *stage_buffers(),
            pltpu.VMEM((probes, count), jnp.float32),
        ],
        compiler_params=PARAMS,
        cost_estimate=cost(count * count),
        name="pair_tile",
    )(left, own, far, acc)


def self_steps(cols):
    steps = []
    for col in cols:
        row = 0
        while row < col + COLS:
            rows = min(ROWS, col + COLS - row)
            steps.append((row, rows, col))
            row += rows
    return steps


def run_self(cols, feats, left_ref, own_ref, out_ref, right, dists, tiles):
    def measure(step, dist):
        row, rows, col = step
        dist[:rows, :] = dot(left_ref[row : row + rows, :], right[:, col : col + COLS], ((1,), (0,)))

    def apply(step, tile):
        row, rows, col = step
        above = min(rows, col - row)
        if above:
            out_ref[:, row : row + above] += dot(own_ref[feats:, col : col + COLS], tile[:above, :], ((1,), (1,)))
        out_ref[:, col : col + COLS] += dot(own_ref[feats:, row : row + rows], tile[:rows, :], ((1,), (0,)))

    run_steps(self_steps(cols), measure, apply, dists, tiles)


def first_kernel(cols, feats, own_ref, left_ref, out_ref, right, dist0, dist1, tile0, tile1):
    left_ref[...] = left_side(own_ref[:feats, :])
    put_right(right, own_ref[:feats, :])
    out_ref[...] = jnp.zeros_like(out_ref)
    run_self(cols, feats, left_ref, own_ref, out_ref, right, (dist0, dist1), (tile0, tile1))


def first_self(own, feats, cols):
    count = own.shape[1]
    probes = own.shape[0] - feats
    return pl.pallas_call(
        functools.partial(first_kernel, cols, feats),
        out_shape=(
            jax.ShapeDtypeStruct((count, DEPTH), jnp.bfloat16),
            jax.ShapeDtypeStruct((probes, count), jnp.float32),
        ),
        in_specs=[VMEM],
        out_specs=[VMEM] * 2,
        scratch_shapes=[pltpu.VMEM((DEPTH, count), jnp.bfloat16), *stage_buffers()],
        compiler_params=PARAMS,
        cost_estimate=cost(sum(step[1] for step in self_steps(cols)) * COLS),
        name="first_self",
    )(own)


def last_kernel(cols, feats, left_ref, own_ref, acc_ref, out_ref, right, dist0, dist1, tile0, tile1):
    put_right(right, own_ref[:feats, :])
    out_ref[...] = acc_ref[...]
    run_self(cols, feats, left_ref, own_ref, out_ref, right, (dist0, dist1), (tile0, tile1))


def last_self(left, own, acc, feats, cols):
    count = own.shape[1]
    return pl.pallas_call(
        functools.partial(last_kernel, cols, feats),
        out_shape=jax.ShapeDtypeStruct(acc.shape, jnp.float32),
        in_specs=[VMEM] * 3,
        out_specs=VMEM,
        scratch_shapes=[pltpu.VMEM((DEPTH, count), jnp.bfloat16), *stage_buffers()],
        compiler_params=PARAMS,
        cost_estimate=cost(sum(step[1] for step in self_steps(cols)) * COLS),
        name="last_self",
    )(left, own, acc)


def move(shard, by):
    count = lax.axis_size("grp") * lax.axis_size("dev")
    return lax.ppermute(shard, ("grp", "dev"), [(i, (i + by) % count) for i in range(count)])


def total(partial):
    for axis in ("dev", "grp"):
        size = lax.axis_size(axis)
        copies = jnp.broadcast_to(partial[None, :], (size, partial.shape[0]))
        partial = jnp.sum(lax.all_to_all(copies, axis, 0, 0), axis=0)
    return partial


def per_device(points, inv_scale, probes, noise):
    feats = points.shape[1]
    wide = probes.T
    scaled = (points.T.astype(jnp.float32) * inv_scale[:, None]).astype(jnp.bfloat16)
    rounded = wide.astype(jnp.bfloat16)
    own = jnp.concatenate([scaled, rounded], axis=0)
    width = lax.axis_size("dev")
    moves = (-1, width, width + 1)
    far = [move(own, by) for by in moves]
    columns = list(range(0, points.shape[0], COLS))
    late = len(columns) // 4
    left, acc = first_self(own, feats, columns[:-late])
    returned = jnp.zeros_like(wide)
    for by, other in zip(moves, far):
        acc, back = pair(left, own, other, acc, feats)
        returned = returned + move(back, -by).astype(jnp.float32)
    acc = last_self(left, own, acc, feats, columns[-late:])
    product = noise[0] * wide + (acc + returned) * 3.0
    count = lax.axis_size("grp") * width * probes.shape[0]
    sums = total(
        jnp.concatenate([jnp.sum(rounded.astype(jnp.float32) * product, axis=1), jnp.sum(product * product, axis=1)])
    )
    mean = sums / count
    curvature, mean_square = jnp.split(mean, 2)
    normalized = product * lax.rsqrt(mean_square + 1e-06)[:, None]
    return (normalized.T, curvature)


def solution(mesh):
    placed = (P(("grp", "dev"), None), P(), P(("grp", "dev"), None), P())
    return jax.shard_map(
        per_device,
        mesh=mesh,
        in_specs=placed,
        out_specs=(P(("grp", "dev"), None), P()),
        check_vma=False,
    )
```

time: 207 us -> 103 us (0.50)
  blocking collectives: 98.3 us -> 34.1 us
  matrix products: 62.2 us -> 0 us
  Pallas kernels: 0 us -> 23 us
  waiting for transfers between devices: 3.84 us -> 10.2 us
  starting transfers between devices: 37.1 us -> 31.4 us
    psum x1 -> x0, blocking collectives: 98.3 us -> none  [per_device(): lax.psum((jnp.sum(wide_probes * product, axis=0), square_local), ('grp',...]
    dot_general x10 -> x0, matrix products: 62.2 us -> none  [the longest x3 36.6 us: matern(): lax.dot_general(left, right, (((1,), (1,)), ((), ())), preferred_element_...]
    all_to_all x0 -> x2, blocking collectives: none -> 34.1 us  [total(): partial = jnp.sum(lax.all_to_all(copies, axis, 0, 0), axis=0)]
    pallas_call x0 -> x5, Pallas kernels: none -> 23 us  [the longest x3 18.9 us: pair(): pl.pallas_call(functools.partial(pair_kernel, feats), out_shape=(jax.Shap...]
    ppermute x9 -> x6, waiting for transfers between devices: 3.84 us -> 10.2 us  [move(): lax.ppermute(shard, ('grp', 'dev'), [(i, (i + by) % count) for i in range...]
    ppermute x9 -> x6, starting transfers between devices: 37.1 us -> 31.4 us  [move(): lax.ppermute(shard, ('grp', 'dev'), [(i, (i + by) % count) for i in range...]
  transfers between devices with their start and end apart: 9 -> 6, of which waited for: 1 -> 3; matrix products, arithmetic and copies ran while one was open for 29% -> 0% of each run, Pallas kernels for 0% -> 16%
where the time goes in v2:
time: 103 us
  blocking collectives  34.1 us (33%)
  starting transfers between devices  31.4 us (30%)
  Pallas kernels  23 us (22%)
  waiting for transfers between devices  10.2 us (10%)
  other arithmetic  2.8 us (3%)
  between operations  1.41 us (1%)
    all_to_all x2, blocking collectives, total(): partial = jnp.sum(lax.all_to_all(copies, axis, 0, 0), axis=0)  34.1 us
    ppermute x6, starting transfers between devices, move(): lax.ppermute(shard, ('grp', 'dev'), [(i, (i + by) % count) for i in range...  31.4 us
    pallas_call x3, Pallas kernels, pair(): pl.pallas_call(functools.partial(pair_kernel, feats), out_shape=(jax.Shap...  18.9 us
    ppermute x6, waiting for transfers between devices, move(): lax.ppermute(shard, ('grp', 'dev'), [(i, (i + by) % count) for i in range...  10.2 us
    pallas_call x1, Pallas kernels, first_self(): pl.pallas_call(functools.partial(first_kernel, cols, feats), out_shape=(j...  2.33 us
  transfers between devices with their start and end apart: 6, of which 3 were waited for; matrix products, arithmetic and copies ran while one was open for 0% of the time, Pallas kernels for 16%

profile of v2, /device:TPU:1, one launch (start us, length us, event | category | flops | bytes accessed | tf_op | source)
XLA Modules:
  0.0 103.0 jit_solution(686556368498501547)
XLA Ops:
  0.6 0.0 copy-start.1
  0.6 0.0 copy-start.2
  0.6 1.0 convert_bitcast_fusion
  1.7 0.0 copy-done.1
  1.7 0.0 copy-done.2
  1.7 0.1 fusion
  1.8 8.8 %collective-permute-start.2 = (bf16[96,2048]{1,0:T(8,128)(2,1)S(1)}, bf16[96,2048]{1,0:T(8,128)(2,1)S(1)}, u32[]{:S(2)}, u32[]{:S(2)}) collective-permute-start(bf16[96,2048]{1,0:T(8,128)(2,1)S(1)} %pad_maximum_fusion.own_ref), channel_id=1, source_target_pairs={{0,511},{1,0},{2,1},{3,2},{4,3},{5,4},{6,5},{7,6},{8,7},{9,8},{10,... | collective-permute-start | bytes 1179656 | tf_op jit(solution)/shard_map/ppermute | solution.py:206
  10.6 1.9 %collective-permute-start.1 = (bf16[96,2048]{1,0:T(8,128)(2,1)S(1)}, bf16[96,2048]{1,0:T(8,128)(2,1)S(1)}, u32[]{:S(2)}, u32[]{:S(2)}) collective-permute-start(bf16[96,2048]{1,0:T(8,128)(2,1)S(1)} %pad_maximum_fusion.own_ref), channel_id=1, source_target_pairs={{0,32},{1,33},{2,34},{3,35},{4,36},{5,37},{6,38},{7,39},{8,40},{9,... | collective-permute-start | bytes 1179656 | tf_op jit(solution)/shard_map/ppermute | solution.py:206
  12.6 2.8 %collective-permute-start = (bf16[96,2048]{1,0:T(8,128)(2,1)S(1)}, bf16[96,2048]{1,0:T(8,128)(2,1)S(1)}, u32[]{:S(2)}, u32[]{:S(2)}) collective-permute-start(bf16[96,2048]{1,0:T(8,128)(2,1)S(1)} %pad_maximum_fusion.own_ref), channel_id=1, source_target_pairs={{0,33},{1,34},{2,35},{3,36},{4,37},{5,38},{6,39},{7,40},{8,41},{9,... | collective-permute-start | bytes 1179656 | tf_op jit(solution)/shard_map/ppermute | solution.py:206
  16.0 2.3 %first_self.1 = (bf16[2048,256]{1,0:T(8,128)(2,1)S(1)}, f32[32,2048]{1,0:T(8,128)S(1)}) custom-call(bf16[96,2048]{1,0:T(8,128)(2,1)S(1)} %pad_maximum_fusion.own_ref), custom_call_target="tpu_custom_call" | custom-call | flops 2064384000 | bytes 1048576 | tf_op jit(solution)/shard_map/first_self/pallas_call | solution.py:169
  18.3 1.2 %collective-permute-done.2.far_ref = bf16[96,2048]{1,0:T(8,128)(2,1)S(1)} collective-permute-done((bf16[96,2048]{1,0:T(8,128)(2,1)S(1)}, bf16[96,2048]{1,0:T(8,128)(2,1)S(1)}, u32[]{:S(2)}, u32[]{:S(2)}) %collective-permute-start.2) | collective-permute-done | bytes 393248 | tf_op jit(solution)/shard_map/ppermute | solution.py:206
  19.5 6.2 %pair_tile.3 = (f32[32,2048]{1,0:T(8,128)S(1)}, bf16[32,2048]{1,0:T(8,128)(2,1)S(1)}) custom-call(bf16[2048,256]{1,0:T(8,128)(2,1)S(1)} %get-tuple-element.10.left_ref, bf16[96,2048]{1,0:T(8,128)(2,1)S(1)} %pad_maximum_fusion.own_ref, bf16[96,2048]{1,0:T(8,128)(2,1)S(1)} %collective-permute-done.2.far_ref, f32[32,2048]{1,0:T(8,128)S(1)} %get-tuple-element.11.acc_ref), custom_call_target="tpu_custom_call" | custom-call | flops 6291456000 | bytes 1048576 | tf_op jit(solution)/shard_map/pair_tile/pallas_call | solution.py:114
  25.8 0.0 collective-permute-done.1.far_ref
  25.8 6.4 %pair_tile.4 = (f32[32,2048]{1,0:T(8,128)S(1)}, bf16[32,2048]{1,0:T(8,128)(2,1)S(1)}) custom-call(bf16[2048,256]{1,0:T(8,128)(2,1)S(1)} %get-tuple-element.10.left_ref, bf16[96,2048]{1,0:T(8,128)(2,1)S(1)} %pad_maximum_fusion.own_ref, bf16[96,2048]{1,0:T(8,128)(2,1)S(1)} %collective-permute-done.1.far_ref, f32[32,2048]{1,0:T(8,128)S(1)} %get-tuple-element.12.acc_ref), custom_call_target="tpu_custom_call" | custom-call | flops 6291456000 | bytes 1048576 | tf_op jit(solution)/shard_map/pair_tile/pallas_call | solution.py:114
  32.2 3.8 %collective-permute-done.far_ref = bf16[96,2048]{1,0:T(8,128)(2,1)S(1)} collective-permute-done((bf16[96,2048]{1,0:T(8,128)(2,1)S(1)}, bf16[96,2048]{1,0:T(8,128)(2,1)S(1)}, u32[]{:S(2)}, u32[]{:S(2)}) %collective-permute-start) | collective-permute-done | bytes 393248 | tf_op jit(solution)/shard_map/ppermute | solution.py:206
  36.0 6.2 %pair_tile.5 = (f32[32,2048]{1,0:T(8,128)S(1)}, bf16[32,2048]{1,0:T(8,128)(2,1)S(1)}) custom-call(bf16[2048,256]{1,0:T(8,128)(2,1)S(1)} %get-tuple-element.10.left_ref, bf16[96,2048]{1,0:T(8,128)(2,1)S(1)} %pad_maximum_fusion.own_ref, bf16[96,2048]{1,0:T(8,128)(2,1)S(1)} %collective-permute-done.far_ref, f32[32,2048]{1,0:T(8,128)S(1)} %get-tuple-element.13.acc_ref), custom_call_target="tpu_custom_call" | custom-call | flops 6291456000 | bytes 1048576 | tf_op jit(solution)/shard_map/pair_tile/pallas_call | solution.py:114
  42.2 14.1 %collective-permute-start.5 = (bf16[32,2048]{1,0:T(8,128)(2,1)S(1)}, bf16[32,2048]{1,0:T(8,128)(2,1)S(1)}, u32[]{:S(2)}, u32[]{:S(2)}) collective-permute-start(bf16[32,2048]{1,0:T(8,128)(2,1)S(1)} %get-tuple-element.17), channel_id=1, source_target_pairs={{0,479},{1,480},{2,481},{3,482},{4,483},{5,484},{6,485},{7,486},{8... | collective-permute-start | bytes 393224 | tf_op jit(solution)/shard_map/ppermute | solution.py:206
  56.3 1.9 %collective-permute-start.4 = (bf16[32,2048]{1,0:T(8,128)(2,1)S(1)}, bf16[32,2048]{1,0:T(8,128)(2,1)S(1)}, u32[]{:S(2)}, u32[]{:S(2)}) collective-permute-start(bf16[32,2048]{1,0:T(8,128)(2,1)S(1)} %get-tuple-element.16), channel_id=1, source_target_pairs={{0,480},{1,481},{2,482},{3,483},{4,484},{5,485},{6,486},{7,487},{8... | collective-permute-start | bytes 393224 | tf_op jit(solution)/shard_map/ppermute | solution.py:206
  58.2 1.9 %collective-permute-start.3 = (bf16[32,2048]{1,0:T(8,128)(2,1)S(1)}, bf16[32,2048]{1,0:T(8,128)(2,1)S(1)}, u32[]{:S(2)}, u32[]{:S(2)}) collective-permute-start(bf16[32,2048]{1,0:T(8,128)(2,1)S(1)} %get-tuple-element.15), channel_id=1, source_target_pairs={{0,1},{1,2},{2,3},{3,4},{4,5},{5,6},{6,7},{7,8},{8,9},{9,10},{10,1... | collective-permute-start | bytes 393224 | tf_op jit(solution)/shard_map/ppermute | solution.py:206
  60.2 0.0 copy-start
  60.2 1.8 %last_self.1 = f32[32,2048]{1,0:T(8,128)S(1)} custom-call(bf16[2048,256]{1,0:T(8,128)(2,1)S(1)} %get-tuple-element.10.left_ref, bf16[96,2048]{1,0:T(8,128)(2,1)S(1)} %pad_maximum_fusion.own_ref, f32[32,2048]{1,0:T(8,128)S(1)} %get-tuple-element.14.acc_ref), custom_call_target="tpu_custom_call" | custom-call | flops 1474560000 | bytes 1048576 | tf_op jit(solution)/shard_map/last_self/pallas_call | solution.py:192
  62.0 0.0 collective-permute-done.5
  62.0 0.0 collective-permute-done.4
  62.0 5.2 %collective-permute-done.3 = bf16[32,2048]{1,0:T(8,128)(2,1)S(1)} collective-permute-done((bf16[32,2048]{1,0:T(8,128)(2,1)S(1)}, bf16[32,2048]{1,0:T(8,128)(2,1)S(1)}, u32[]{:S(2)}, u32[]{:S(2)}) %collective-permute-start.3) | collective-permute-done | bytes 131104 | tf_op jit(solution)/shard_map/ppermute | solution.py:206
  67.2 0.0 copy-done
  67.2 0.2 multiply_reduce_fusion.1
  67.5 0.1 pad_maximum_fusion.1
  67.5 22.1 %all_to_all.12 = f32[32,1,64]{2,1,0:T(1,128)S(1)} all-to-all(f32[32,1,64]{2,1,0:T(1,128)S(1)} %broadcast_in_dim.4), channel_id=1, replica_groups=mesh['grp'=16,'dev'=32] {'dev'}, dimensions={0} | all-to-all | bytes 16384 | tf_op jit(solution)/shard_map/all_to_all | solution.py:213
  89.7 12.0 %all_to_all.13 = f32[16,1,64]{2,1,0:T(1,128)S(1)} all-to-all(f32[16,1,64]{2,1,0:T(1,128)S(1)} %broadcast_in_dim.5), channel_id=1, replica_groups=mesh['grp'=16,'dev'=32] {'grp'}, dimensions={0} | all-to-all | bytes 8192 | tf_op jit(solution)/shard_map/all_to_all | solution.py:213
  101.7 0.5 fusion.1
  102.2 0.8 multiply_bitcast_fusion
  (6 shorter events, 0.1 us)
Async XLA Ops:
  0.6 1.0 %copy-start.1 = (bf16[2048,64]{0,1:T(8,128)(2,1)S(1)}, bf16[2048,64]{0,1:T(8,128)(2,1)}, u32[]{:S(2)}) copy-start(bf16[2048,64]{0,1:T(8,128)(2,1)} %param.4) | copy-start | bytes 786436
  0.6 1.0 %copy-start.2 = (f32[64]{0:T(128)S(1)}, f32[64]{0:T(128)}, u32[]{:S(2)}) copy-start(f32[64]{0:T(128)} %param.5) | copy-start | bytes 772
  1.8 17.7 %collective-permute-start.2 = (bf16[96,2048]{1,0:T(8,128)(2,1)S(1)}, bf16[96,2048]{1,0:T(8,128)(2,1)S(1)}, u32[]{:S(2)}, u32[]{:S(2)}) collective-permute-start(bf16[96,2048]{1,0:T(8,128)(2,1)S(1)} %pad_maximum_fusion.own_ref), channel_id=1, source_target_pairs={{0,511},{1,0},{2,1},{3,2},{4,3},{5,4},{6,5},{7,6},{8,7},{9,8},{10,... | collective-permute-start | bytes 1179656 | tf_op jit(solution)/shard_map/ppermute | solution.py:206
  10.6 15.1 %collective-permute-start.1 = (bf16[96,2048]{1,0:T(8,128)(2,1)S(1)}, bf16[96,2048]{1,0:T(8,128)(2,1)S(1)}, u32[]{:S(2)}, u32[]{:S(2)}) collective-permute-start(bf16[96,2048]{1,0:T(8,128)(2,1)S(1)} %pad_maximum_fusion.own_ref), channel_id=1, source_target_pairs={{0,32},{1,33},{2,34},{3,35},{4,36},{5,37},{6,38},{7,39},{8,40},{9,... | collective-permute-start | bytes 1179656 | tf_op jit(solution)/shard_map/ppermute | solution.py:206
  12.6 23.4 %collective-permute-start = (bf16[96,2048]{1,0:T(8,128)(2,1)S(1)}, bf16[96,2048]{1,0:T(8,128)(2,1)S(1)}, u32[]{:S(2)}, u32[]{:S(2)}) collective-permute-start(bf16[96,2048]{1,0:T(8,128)(2,1)S(1)} %pad_maximum_fusion.own_ref), channel_id=1, source_target_pairs={{0,33},{1,34},{2,35},{3,36},{4,37},{5,38},{6,39},{7,40},{8,41},{9,... | collective-permute-start | bytes 1179656 | tf_op jit(solution)/shard_map/ppermute | solution.py:206
  42.2 19.8 %collective-permute-start.5 = (bf16[32,2048]{1,0:T(8,128)(2,1)S(1)}, bf16[32,2048]{1,0:T(8,128)(2,1)S(1)}, u32[]{:S(2)}, u32[]{:S(2)}) collective-permute-start(bf16[32,2048]{1,0:T(8,128)(2,1)S(1)} %get-tuple-element.17), channel_id=1, source_target_pairs={{0,479},{1,480},{2,481},{3,482},{4,483},{5,484},{6,485},{7,486},{8... | collective-permute-start | bytes 393224 | tf_op jit(solution)/shard_map/ppermute | solution.py:206
  56.3 5.7 %collective-permute-start.4 = (bf16[32,2048]{1,0:T(8,128)(2,1)S(1)}, bf16[32,2048]{1,0:T(8,128)(2,1)S(1)}, u32[]{:S(2)}, u32[]{:S(2)}) collective-permute-start(bf16[32,2048]{1,0:T(8,128)(2,1)S(1)} %get-tuple-element.16), channel_id=1, source_target_pairs={{0,480},{1,481},{2,482},{3,483},{4,484},{5,485},{6,486},{7,487},{8... | collective-permute-start | bytes 393224 | tf_op jit(solution)/shard_map/ppermute | solution.py:206
  58.2 9.0 %collective-permute-start.3 = (bf16[32,2048]{1,0:T(8,128)(2,1)S(1)}, bf16[32,2048]{1,0:T(8,128)(2,1)S(1)}, u32[]{:S(2)}, u32[]{:S(2)}) collective-permute-start(bf16[32,2048]{1,0:T(8,128)(2,1)S(1)} %get-tuple-element.15), channel_id=1, source_target_pairs={{0,1},{1,2},{2,3},{3,4},{4,5},{5,6},{6,7},{7,8},{8,9},{9,10},{10,1... | collective-permute-start | bytes 393224 | tf_op jit(solution)/shard_map/ppermute | solution.py:206
  60.2 7.1 %copy-start = (f32[2048,32]{0,1:T(8,128)S(1)}, f32[2048,32]{0,1:T(8,128)}, u32[]{:S(2)}) copy-start(f32[2048,32]{0,1:T(8,128)} %param.6) | copy-start | bytes 786436

commit v3 on v2

--- a/solution.py
+++ b/solution.py
@@ -13,6 +13,7 @@
 COLS = 256
 ROWS = 512
 VMEM = pl.BlockSpec(memory_space=pltpu.VMEM)
+COST = pl.CostEstimate(flops=1000, bytes_accessed=1000, transcendentals=0)
 PARAMS = pltpu.CompilerParams(vmem_limit_bytes=32 * 2**20)
 
 
@@ -76,24 +77,30 @@
             measure(steps[k], dists[k % 2])
 
 
-def pair_kernel(feats, left_ref, own_ref, far_ref, acc_ref, out_ref, back_ref, right, dist0, dist1, tile0, tile1, back):
-    count = own_ref.shape[1]
-    put_right(right, far_ref[:feats, :])
-    out_ref[...] = acc_ref[...]
-    back[...] = jnp.zeros_like(back)
+def pair_kernel(feats, names, *refs):
+    ref = dict(zip(names, refs))
+    rows_ref, cols_ref, right, out, back = (ref[name] for name in ("rows", "cols", "right", "out", "back"))
+    count = rows_ref.shape[1]
+    left = ref["made"] if "made" in ref else ref["left"]
+    if "made" in ref:
+        left[...] = left_side(rows_ref[:feats, :])
+    put_right(right, cols_ref[:feats, :])
+    out[...] = ref["acc"][...]
+    back[...] = ref["back_acc"][...] if "back_acc" in ref else jnp.zeros_like(back)
 
     def measure(step, dist):
         row, rows, col = step
-        dist[...] = dot(left_ref[row : row + rows, :], right[:, col : col + COLS], ((1,), (0,)))
+        dist[...] = dot(left[row : row + rows, :], right[:, col : col + COLS], ((1,), (0,)))
 
     def apply(step, tile):
         row, rows, col = step
-        out_ref[:, row : row + rows] += dot(far_ref[feats:, col : col + COLS], tile[...], ((1,), (1,)))
-        back[:, col : col + COLS] += dot(own_ref[feats:, row : row + rows], tile[...], ((1,), (0,)))
+        out[:, row : row + rows] += dot(cols_ref[feats:, col : col + COLS], tile[...], ((1,), (1,)))
+        back[:, col : col + COLS] += dot(rows_ref[feats:, row : row + rows], tile[...], ((1,), (0,)))
 
     steps = [(row, ROWS, col) for col in range(0, count, COLS) for row in range(0, count, ROWS)]
-    run_steps(steps, measure, apply, (dist0, dist1), (tile0, tile1))
-    back_ref[...] = back[...].astype(back_ref.dtype)
+    run_steps(steps, measure, apply, (ref["dist0"], ref["dist1"]), (ref["tile0"], ref["tile1"]))
+    ref["out_ref"][...] = out[...].astype(ref["out_ref"].dtype)
+    ref["back_ref"][...] = back[...].astype(ref["back_ref"].dtype)
 
 
 def stage_buffers():
@@ -105,29 +112,28 @@
     ]
 
 
-def cost(elements):
-    return pl.CostEstimate(flops=elements * 1500, bytes_accessed=2**20, transcendentals=2 * elements)
-
-
-def pair(left, own, far, acc, feats):
+def pair(rows, cols, acc, feats, left=None, back_acc=None, out_dtype=jnp.float32, back_dtype=jnp.float32):
     probes, count = acc.shape
+    given = {"left": left, "rows": rows, "cols": cols, "acc": acc, "back_acc": back_acc}
+    given = {name: value for name, value in given.items() if value is not None}
+    made = {"right": pltpu.VMEM((DEPTH, count), jnp.bfloat16)}
+    if left is None:
+        made["made"] = pltpu.VMEM((count, DEPTH), jnp.bfloat16)
+    made["out"] = made["back"] = pltpu.VMEM((probes, count), jnp.float32)
+    names = [*given, "out_ref", "back_ref", *made, "dist0", "dist1", "tile0", "tile1"]
     return pl.pallas_call(
-        functools.partial(pair_kernel, feats),
+        functools.partial(pair_kernel, feats, names),
         out_shape=(
-            jax.ShapeDtypeStruct((probes, count), jnp.float32),
-            jax.ShapeDtypeStruct((probes, count), jnp.bfloat16),
+            jax.ShapeDtypeStruct((probes, count), out_dtype),
+            jax.ShapeDtypeStruct((probes, count), back_dtype),
         ),
-        in_specs=[VMEM] * 4,
+        in_specs=[VMEM] * len(given),
         out_specs=[VMEM] * 2,
-        scratch_shapes=[
-            pltpu.VMEM((DEPTH, count), jnp.bfloat16),
-            *stage_buffers(),
-            pltpu.VMEM((probes, count), jnp.float32),
-        ],
+        scratch_shapes=[*made.values(), *stage_buffers()],
         compiler_params=PARAMS,
-        cost_estimate=cost(count * count),
+        cost_estimate=COST,
         name="pair_tile",
-    )(left, own, far, acc)
+    )(*given.values())
 
 
 def self_steps(cols):
@@ -176,29 +182,29 @@
         out_specs=[VMEM] * 2,
         scratch_shapes=[pltpu.VMEM((DEPTH, count), jnp.bfloat16), *stage_buffers()],
         compiler_params=PARAMS,
-        cost_estimate=cost(sum(step[1] for step in self_steps(cols)) * COLS),
+        cost_estimate=COST,
         name="first_self",
     )(own)
 
 
-def last_kernel(cols, feats, left_ref, own_ref, acc_ref, out_ref, right, dist0, dist1, tile0, tile1):
+def last_kernel(cols, feats, left_ref, own_ref, acc_ref, more_ref, out_ref, right, dist0, dist1, tile0, tile1):
     put_right(right, own_ref[:feats, :])
-    out_ref[...] = acc_ref[...]
+    out_ref[...] = acc_ref[...] + more_ref[...].astype(jnp.float32)
     run_self(cols, feats, left_ref, own_ref, out_ref, right, (dist0, dist1), (tile0, tile1))
 
 
-def last_self(left, own, acc, feats, cols):
+def last_self(left, own, acc, more, feats, cols):
     count = own.shape[1]
     return pl.pallas_call(
         functools.partial(last_kernel, cols, feats),
         out_shape=jax.ShapeDtypeStruct(acc.shape, jnp.float32),
-        in_specs=[VMEM] * 3,
+        in_specs=[VMEM] * 4,
         out_specs=VMEM,
         scratch_shapes=[pltpu.VMEM((DEPTH, count), jnp.bfloat16), *stage_buffers()],
         compiler_params=PARAMS,
-        cost_estimate=cost(sum(step[1] for step in self_steps(cols)) * COLS),
+        cost_estimate=COST,
         name="last_self",
-    )(left, own, acc)
+    )(left, own, acc, more)
 
 
 def move(shard, by):
@@ -221,17 +227,18 @@
     rounded = wide.astype(jnp.bfloat16)
     own = jnp.concatenate([scaled, rounded], axis=0)
     width = lax.axis_size("dev")
-    moves = (-1, width, width + 1)
-    far = [move(own, by) for by in moves]
+    near = move(own, 1)
+    wide_far = move(own, -width)
     columns = list(range(0, points.shape[0], COLS))
     late = len(columns) // 4
     left, acc = first_self(own, feats, columns[:-late])
-    returned = jnp.zeros_like(wide)
-    for by, other in zip(moves, far):
-        acc, back = pair(left, own, other, acc, feats)
-        returned = returned + move(back, -by).astype(jnp.float32)
-    acc = last_self(left, own, acc, feats, columns[-late:])
-    product = noise[0] * wide + (acc + returned) * 3.0
+    acc, near_acc = pair(own, near, acc, feats, left=left)
+    to_near, far_acc = pair(near, wide_far, near_acc, feats, out_dtype=jnp.bfloat16)
+    from_near = move(to_near, -1)
+    acc, to_far = pair(own, wide_far, acc, feats, left=left, back_acc=far_acc, back_dtype=jnp.bfloat16)
+    from_far = move(to_far, width)
+    acc = last_self(left, own, acc, from_near, feats, columns[-late:])
+    product = noise[0] * wide + (acc + from_far.astype(jnp.float32)) * 3.0
     count = lax.axis_size("grp") * width * probes.shape[0]
     sums = total(
         jnp.concatenate([jnp.sum(rounded.astype(jnp.float32) * product, axis=1), jnp.sum(product * product, axis=1)])

time: 103 us -> 95.4 us (0.926)
  blocking collectives: 34.1 us -> 27.2 us
  starting transfers between devices: 31.4 us -> 27 us
  waiting for transfers between devices: 10.2 us -> 13.1 us
    all_to_all x2, blocking collectives: 34.1 us -> 27.2 us  [total(): partial = jnp.sum(lax.all_to_all(copies, axis, 0, 0), axis=0)]
    ppermute x6 -> x4, starting transfers between devices: 31.4 us -> 27 us  [move(): lax.ppermute(shard, ('grp', 'dev'), [(i, (i + by) % count) for i in range...]
    ppermute x6 -> x4, waiting for transfers between devices: 10.2 us -> 13.1 us  [move(): lax.ppermute(shard, ('grp', 'dev'), [(i, (i + by) % count) for i in range...]
  transfers between devices with their start and end apart: 6 -> 4, of which waited for: 3 -> 2; matrix products, arithmetic and copies ran while one was open for 0% -> 0% of each run, Pallas kernels for 16% -> 17%
where the time goes in v3:
time: 95.4 us; the launch traced here: 95.1 us
  blocking collectives  27.2 us (29%)
  starting transfers between devices  27 us (28%)
  Pallas kernels  23.6 us (25%)
  waiting for transfers between devices  13.1 us (14%)
  other arithmetic  2.77 us (3%)
  between operations  1.38 us (1%)
    all_to_all x2, blocking collectives, total(): partial = jnp.sum(lax.all_to_all(copies, axis, 0, 0), axis=0)  27.2 us
    ppermute x4, starting transfers between devices, move(): lax.ppermute(shard, ('grp', 'dev'), [(i, (i + by) % count) for i in range...  27 us
    pallas_call x3, Pallas kernels, pair(): pl.pallas_call(functools.partial(pair_kernel, feats, names), out_shape=(j...  19.5 us
    ppermute x4, waiting for transfers between devices, move(): lax.ppermute(shard, ('grp', 'dev'), [(i, (i + by) % count) for i in range...  13.1 us
    pallas_call x1, Pallas kernels, first_self(): pl.pallas_call(functools.partial(first_kernel, cols, feats), out_shape=(j...  2.33 us
  transfers between devices with their start and end apart: 4, of which 2 were waited for; matrix products, arithmetic and copies ran while one was open for 0% of the time, Pallas kernels for 17%

profile of v3, /device:TPU:1, one launch (start us, length us, event | category | flops | bytes accessed | tf_op | source)
XLA Modules:
  0.0 95.1 jit_solution(14834546344627045750)
XLA Ops:
  0.6 0.0 copy-start.1
  0.6 0.0 copy-start.2
  0.6 1.0 %convert_bitcast_fusion = bf16[32,2048]{1,0:T(8,128)(2,1)S(1)} fusion(f32[2048,32]{0,1:T(8,128)} %param.6), kind=kLoop, calls=%fused_computation.7 | loop fusion | flops 65536 | bytes 393216 | tf_op jit(solution)/shard_map/convert_element_type | solution.py:227
  1.7 0.0 copy-done.1
  1.7 0.0 copy-done.2
  1.7 0.1 fusion
  1.8 7.2 %collective-permute-start.1 = (bf16[96,2048]{1,0:T(8,128)(2,1)S(1)}, bf16[96,2048]{1,0:T(8,128)(2,1)S(1)}, u32[]{:S(2)}, u32[]{:S(2)}) collective-permute-start(bf16[96,2048]{1,0:T(8,128)(2,1)S(1)} %pad_maximum_fusion.own_ref.refs_1_), channel_id=1, source_target_pairs={{0,1},{1,2},{2,3},{3,4},{4,5},{5,6},{6,7},{7,8},{8,9},{9,10},{10,1... | collective-permute-start | bytes 1179656 | tf_op jit(solution)/shard_map/ppermute | solution.py:212
  9.0 6.9 %collective-permute-start = (bf16[96,2048]{1,0:T(8,128)(2,1)S(1)}, bf16[96,2048]{1,0:T(8,128)(2,1)S(1)}, u32[]{:S(2)}, u32[]{:S(2)}) collective-permute-start(bf16[96,2048]{1,0:T(8,128)(2,1)S(1)} %pad_maximum_fusion.own_ref.refs_1_), channel_id=1, source_target_pairs={{0,480},{1,481},{2,482},{3,483},{4,484},{5,485},{6,486},{7,487},{8... | collective-permute-start | bytes 1179656 | tf_op jit(solution)/shard_map/ppermute | solution.py:212
  16.0 2.3 %first_self.1 = (bf16[2048,256]{1,0:T(8,128)(2,1)S(1)}, f32[32,2048]{1,0:T(8,128)S(1)}) custom-call(bf16[96,2048]{1,0:T(8,128)(2,1)S(1)} %pad_maximum_fusion.own_ref.refs_1_), custom_call_target="tpu_custom_call" | custom-call | flops 1000 | bytes 1000 | tf_op jit(solution)/shard_map/first_self/pallas_call | solution.py:175
  18.3 8.1 %collective-permute-done.1.refs_2_.refs_0_ = bf16[96,2048]{1,0:T(8,128)(2,1)S(1)} collective-permute-done((bf16[96,2048]{1,0:T(8,128)(2,1)S(1)}, bf16[96,2048]{1,0:T(8,128)(2,1)S(1)}, u32[]{:S(2)}, u32[]{:S(2)}) %collective-permute-start.1) | collective-permute-done | bytes 393248 | tf_op jit(solution)/shard_map/ppermute | solution.py:212
  26.4 6.2 %pair_tile.3 = (f32[32,2048]{1,0:T(8,128)S(1)}, f32[32,2048]{1,0:T(8,128)S(1)}) custom-call(bf16[2048,256]{1,0:T(8,128)(2,1)S(1)} %get-tuple-element.10.refs_0_.left_ref, bf16[96,2048]{1,0:T(8,128)(2,1)S(1)} %pad_maximum_fusion.own_ref.refs_1_, bf16[96,2048]{1,0:T(8,128)(2,1)S(1)} %collective-permute-done.1.refs_2_.refs_0_, ...), custom_call_target="tpu_custom_call" | custom-call | flops 1000 | bytes 1000 | tf_op jit(solution)/shard_map/pair_tile/pallas_call | solution.py:124
  32.6 0.0 collective-permute-done.refs_1_.refs_2_
  32.6 7.0 %pair_tile.4 = (bf16[32,2048]{1,0:T(8,128)(2,1)S(1)}, f32[32,2048]{1,0:T(8,128)S(1)}) custom-call(bf16[96,2048]{1,0:T(8,128)(2,1)S(1)} %collective-permute-done.1.refs_2_.refs_0_, bf16[96,2048]{1,0:T(8,128)(2,1)S(1)} %collective-permute-done.refs_1_.refs_2_, f32[32,2048]{1,0:T(8,128)S(1)} %get-tuple-element.13.refs_2_), custom_call_target="tpu_custom_call" | custom-call | flops 1000 | bytes 1000 | tf_op jit(solution)/shard_map/pair_tile/pallas_call | solution.py:124
  39.6 1.9 %collective-permute-start.2 = (bf16[32,2048]{1,0:T(8,128)(2,1)S(1)}, bf16[32,2048]{1,0:T(8,128)(2,1)S(1)}, u32[]{:S(2)}, u32[]{:S(2)}) collective-permute-start(bf16[32,2048]{1,0:T(8,128)(2,1)S(1)} %get-tuple-element.16), channel_id=1, source_target_pairs={{0,511},{1,0},{2,1},{3,2},{4,3},{5,4},{6,5},{7,6},{8,7},{9,8},{10,... | collective-permute-start | bytes 393224 | tf_op jit(solution)/shard_map/ppermute | solution.py:212
  41.5 6.3 %pair_tile.5 = (f32[32,2048]{1,0:T(8,128)S(1)}, bf16[32,2048]{1,0:T(8,128)(2,1)S(1)}) custom-call(bf16[2048,256]{1,0:T(8,128)(2,1)S(1)} %get-tuple-element.10.refs_0_.left_ref, bf16[96,2048]{1,0:T(8,128)(2,1)S(1)} %pad_maximum_fusion.own_ref.refs_1_, bf16[96,2048]{1,0:T(8,128)(2,1)S(1)} %collective-permute-done.refs_1_.refs_2_, ...), custom_call_target="tpu_custom_call" | custom-call | flops 1000 | bytes 1000 | tf_op jit(solution)/shard_map/pair_tile/pallas_call | solution.py:124
  47.8 11.0 %collective-permute-start.3 = (bf16[32,2048]{1,0:T(8,128)(2,1)S(1)}, bf16[32,2048]{1,0:T(8,128)(2,1)S(1)}, u32[]{:S(2)}, u32[]{:S(2)}) collective-permute-start(bf16[32,2048]{1,0:T(8,128)(2,1)S(1)} %get-tuple-element.17), channel_id=1, source_target_pairs={{0,32},{1,33},{2,34},{3,35},{4,36},{5,37},{6,38},{7,39},{8,40},{9,... | collective-permute-start | bytes 393224 | tf_op jit(solution)/shard_map/ppermute | solution.py:212
  59.5 0.0 collective-permute-done.2.more_ref
  59.5 0.0 copy-start
  59.5 1.8 %last_self.1 = f32[32,2048]{1,0:T(8,128)S(1)} custom-call(bf16[2048,256]{1,0:T(8,128)(2,1)S(1)} %get-tuple-element.10.refs_0_.left_ref, bf16[96,2048]{1,0:T(8,128)(2,1)S(1)} %pad_maximum_fusion.own_ref.refs_1_, f32[32,2048]{1,0:T(8,128)S(1)} %get-tuple-element.15.acc_ref, bf16[32,2048]{1,0:T(8,128)(2,1)S(1)} %collective-permute-done.2.more_ref), custom_call_target="tpu_custom_call" | custom-call | flops 1000 | bytes 1000 | tf_op jit(solution)/shard_map/last_self/pallas_call | solution.py:198
  61.3 5.0 %collective-permute-done.3 = bf16[32,2048]{1,0:T(8,128)(2,1)S(1)} collective-permute-done((bf16[32,2048]{1,0:T(8,128)(2,1)S(1)}, bf16[32,2048]{1,0:T(8,128)(2,1)S(1)}, u32[]{:S(2)}, u32[]{:S(2)}) %collective-permute-start.3) | collective-permute-done | bytes 131104 | tf_op jit(solution)/shard_map/ppermute | solution.py:212
  66.3 0.0 copy-done
  66.3 0.2 multiply_reduce_fusion.1
  66.5 0.1 pad_maximum_fusion.1
  66.6 13.1 %all_to_all.12 = f32[32,1,64]{2,1,0:T(1,128)S(1)} all-to-all(f32[32,1,64]{2,1,0:T(1,128)S(1)} %broadcast_in_dim.4), channel_id=1, replica_groups=mesh['grp'=16,'dev'=32] {'dev'}, dimensions={0} | all-to-all | bytes 16384 | tf_op jit(solution)/shard_map/all_to_all | solution.py:219
  79.7 14.0 %all_to_all.13 = f32[16,1,64]{2,1,0:T(1,128)S(1)} all-to-all(f32[16,1,64]{2,1,0:T(1,128)S(1)} %broadcast_in_dim.5), channel_id=1, replica_groups=mesh['grp'=16,'dev'=32] {'grp'}, dimensions={0} | all-to-all | bytes 8192 | tf_op jit(solution)/shard_map/all_to_all | solution.py:219
  93.8 0.5 fusion.1
  94.3 0.8 multiply_bitcast_fusion
  (6 shorter events, 0.1 us)
Async XLA Ops:
  0.6 1.0 %copy-start.1 = (bf16[2048,64]{0,1:T(8,128)(2,1)S(1)}, bf16[2048,64]{0,1:T(8,128)(2,1)}, u32[]{:S(2)}) copy-start(bf16[2048,64]{0,1:T(8,128)(2,1)} %param.4) | copy-start | bytes 786436
  0.6 1.0 %copy-start.2 = (f32[64]{0:T(128)S(1)}, f32[64]{0:T(128)}, u32[]{:S(2)}) copy-start(f32[64]{0:T(128)} %param.5) | copy-start | bytes 772
  1.8 24.5 %collective-permute-start.1 = (bf16[96,2048]{1,0:T(8,128)(2,1)S(1)}, bf16[96,2048]{1,0:T(8,128)(2,1)S(1)}, u32[]{:S(2)}, u32[]{:S(2)}) collective-permute-start(bf16[96,2048]{1,0:T(8,128)(2,1)S(1)} %pad_maximum_fusion.own_ref.refs_1_), channel_id=1, source_target_pairs={{0,1},{1,2},{2,3},{3,4},{4,5},{5,6},{6,7},{7,8},{8,9},{9,10},{10,1... | collective-permute-start | bytes 1179656 | tf_op jit(solution)/shard_map/ppermute | solution.py:212
  9.0 23.6 %collective-permute-start = (bf16[96,2048]{1,0:T(8,128)(2,1)S(1)}, bf16[96,2048]{1,0:T(8,128)(2,1)S(1)}, u32[]{:S(2)}, u32[]{:S(2)}) collective-permute-start(bf16[96,2048]{1,0:T(8,128)(2,1)S(1)} %pad_maximum_fusion.own_ref.refs_1_), channel_id=1, source_target_pairs={{0,480},{1,481},{2,482},{3,483},{4,484},{5,485},{6,486},{7,487},{8... | collective-permute-start | bytes 1179656 | tf_op jit(solution)/shard_map/ppermute | solution.py:212
  39.6 19.9 %collective-permute-start.2 = (bf16[32,2048]{1,0:T(8,128)(2,1)S(1)}, bf16[32,2048]{1,0:T(8,128)(2,1)S(1)}, u32[]{:S(2)}, u32[]{:S(2)}) collective-permute-start(bf16[32,2048]{1,0:T(8,128)(2,1)S(1)} %get-tuple-element.16), channel_id=1, source_target_pairs={{0,511},{1,0},{2,1},{3,2},{4,3},{5,4},{6,5},{7,6},{8,7},{9,8},{10,... | collective-permute-start | bytes 393224 | tf_op jit(solution)/shard_map/ppermute | solution.py:212
  47.8 18.5 %collective-permute-start.3 = (bf16[32,2048]{1,0:T(8,128)(2,1)S(1)}, bf16[32,2048]{1,0:T(8,128)(2,1)S(1)}, u32[]{:S(2)}, u32[]{:S(2)}) collective-permute-start(bf16[32,2048]{1,0:T(8,128)(2,1)S(1)} %get-tuple-element.17), channel_id=1, source_target_pairs={{0,32},{1,33},{2,34},{3,35},{4,36},{5,37},{6,38},{7,39},{8,40},{9,... | collective-permute-start | bytes 393224 | tf_op jit(solution)/shard_map/ppermute | solution.py:212
  59.5 6.8 %copy-start = (f32[2048,32]{0,1:T(8,128)S(1)}, f32[2048,32]{0,1:T(8,128)}, u32[]{:S(2)}) copy-start(f32[2048,32]{0,1:T(8,128)} %param.6) | copy-start | bytes 786436

commit v4 on v3

--- a/solution.py
+++ b/solution.py
@@ -162,10 +162,11 @@
     run_steps(self_steps(cols), measure, apply, dists, tiles)
 
 
-def first_kernel(cols, feats, own_ref, left_ref, out_ref, right, dist0, dist1, tile0, tile1):
+def first_kernel(cols, feats, own_ref, left_ref, out_ref, copy_ref, right, dist0, dist1, tile0, tile1):
     left_ref[...] = left_side(own_ref[:feats, :])
     put_right(right, own_ref[:feats, :])
     out_ref[...] = jnp.zeros_like(out_ref)
+    copy_ref[...] = own_ref[...]
     run_self(cols, feats, left_ref, own_ref, out_ref, right, (dist0, dist1), (tile0, tile1))
 
 
@@ -177,9 +178,10 @@
         out_shape=(
             jax.ShapeDtypeStruct((count, DEPTH), jnp.bfloat16),
             jax.ShapeDtypeStruct((probes, count), jnp.float32),
+            jax.ShapeDtypeStruct(own.shape, own.dtype),
         ),
         in_specs=[VMEM],
-        out_specs=[VMEM] * 2,
+        out_specs=[VMEM] * 3,
         scratch_shapes=[pltpu.VMEM((DEPTH, count), jnp.bfloat16), *stage_buffers()],
         compiler_params=PARAMS,
         cost_estimate=COST,
@@ -205,6 +207,22 @@
         cost_estimate=COST,
         name="last_self",
     )(left, own, acc, more)
+
+
+def after_kernel(first_ref, own_ref, copy_ref):
+    copy_ref[...] = own_ref[...]
+
+
+def after(first, own):
+    return pl.pallas_call(
+        after_kernel,
+        out_shape=jax.ShapeDtypeStruct(own.shape, own.dtype),
+        in_specs=[VMEM] * 2,
+        out_specs=VMEM,
+        compiler_params=PARAMS,
+        cost_estimate=COST,
+        name="after",
+    )(first, own)
 
 
 def move(shard, by):
@@ -228,10 +246,10 @@
     own = jnp.concatenate([scaled, rounded], axis=0)
     width = lax.axis_size("dev")
     near = move(own, 1)
-    wide_far = move(own, -width)
     columns = list(range(0, points.shape[0], COLS))
     late = len(columns) // 4
-    left, acc = first_self(own, feats, columns[:-late])
+    left, acc, again = first_self(own, feats, columns[:-late])
+    wide_far = move(after(near, again), -width)
     acc, near_acc = pair(own, near, acc, feats, left=left)
     to_near, far_acc = pair(near, wide_far, near_acc, feats, out_dtype=jnp.bfloat16)
     from_near = move(to_near, -1)

time: 95.4 us -> 92.8 us (0.973)
  waiting for transfers between devices: 13.1 us -> 7.14 us
  starting transfers between devices: 27 us -> 30.9 us
    ppermute x4, waiting for transfers between devices: 13.1 us -> 7.14 us  [move(): lax.ppermute(shard, ('grp', 'dev'), [(i, (i + by) % count) for i in range...]
    ppermute x4, starting transfers between devices: 27 us -> 30.9 us  [move(): lax.ppermute(shard, ('grp', 'dev'), [(i, (i + by) % count) for i in range...]
  transfers between devices with their start and end apart: 4 -> 4, of which waited for: 2 -> 2; matrix products, arithmetic and copies ran while one was open for 0% -> 0% of each run, Pallas kernels for 17% -> 18%
where the time goes in v4:
time: 92.8 us; the launch traced here: 92.5 us
  starting transfers between devices  30.9 us (33%)
  blocking collectives  26.5 us (29%)
  Pallas kernels  23.7 us (26%)
  waiting for transfers between devices  7.14 us (8%)
  other arithmetic  2.77 us (3%)
  between operations  1.39 us (1%)
    ppermute x4, starting transfers between devices, move(): lax.ppermute(shard, ('grp', 'dev'), [(i, (i + by) % count) for i in range...  30.9 us
    all_to_all x2, blocking collectives, total(): partial = jnp.sum(lax.all_to_all(copies, axis, 0, 0), axis=0)  26.5 us
    pallas_call x3, Pallas kernels, pair(): pl.pallas_call(functools.partial(pair_kernel, feats, names), out_shape=(j...  19.5 us
    ppermute x4, waiting for transfers between devices, move(): lax.ppermute(shard, ('grp', 'dev'), [(i, (i + by) % count) for i in range...  7.14 us
    pallas_call x1, Pallas kernels, first_self(): pl.pallas_call(functools.partial(first_kernel, cols, feats), out_shape=(j...  2.34 us
  transfers between devices with their start and end apart: 4, of which 2 were waited for; matrix products, arithmetic and copies ran while one was open for 0% of the time, Pallas kernels for 18%

profile of v4, /device:TPU:1, one launch (start us, length us, event | category | flops | bytes accessed | tf_op | source)
XLA Modules:
  0.0 92.5 jit_solution(14750849087534532921)
XLA Ops:
  0.6 0.0 copy-start.1
  0.6 0.0 copy-start.2
  0.6 1.0 %convert_bitcast_fusion = bf16[32,2048]{1,0:T(8,128)(2,1)S(1)} fusion(f32[2048,32]{0,1:T(8,128)} %param.6), kind=kLoop, calls=%fused_computation.7 | loop fusion | flops 65536 | bytes 393216 | tf_op jit(solution)/shard_map/convert_element_type | solution.py:245
  1.7 0.0 copy-done.1
  1.7 0.0 copy-done.2
  1.7 0.1 fusion
  1.8 7.2 %collective-permute-start = (bf16[96,2048]{1,0:T(8,128)(2,1)S(1)}, bf16[96,2048]{1,0:T(8,128)(2,1)S(1)}, u32[]{:S(2)}, u32[]{:S(2)}) collective-permute-start(bf16[96,2048]{1,0:T(8,128)(2,1)S(1)} %pad_maximum_fusion.own_ref.refs_1_), channel_id=1, source_target_pairs={{0,1},{1,2},{2,3},{3,4},{4,5},{5,6},{6,7},{7,8},{8,9},{9,10},{10,1... | collective-permute-start | bytes 1179656 | tf_op jit(solution)/shard_map/ppermute | solution.py:230
  9.0 2.3 %first_self.1 = (bf16[2048,256]{1,0:T(8,128)(2,1)S(1)}, f32[32,2048]{1,0:T(8,128)S(1)}, bf16[96,2048]{1,0:T(8,128)(2,1)S(1)}) custom-call(bf16[96,2048]{1,0:T(8,128)(2,1)S(1)} %pad_maximum_fusion.own_ref.refs_1_), custom_call_target="tpu_custom_call" | custom-call | flops 1000 | bytes 1000 | tf_op jit(solution)/shard_map/first_self/pallas_call | solution.py:176
  11.4 2.4 %collective-permute-done.first_ref.refs_2_.refs_0_ = bf16[96,2048]{1,0:T(8,128)(2,1)S(1)} collective-permute-done((bf16[96,2048]{1,0:T(8,128)(2,1)S(1)}, bf16[96,2048]{1,0:T(8,128)(2,1)S(1)}, u32[]{:S(2)}, u32[]{:S(2)}) %collective-permute-start) | collective-permute-done | bytes 393248 | tf_op jit(solution)/shard_map/ppermute | solution.py:230
  13.8 10.4 %collective-permute-start.1 = (bf16[96,2048]{1,0:T(8,128)(2,1)S(1)}, bf16[96,2048]{1,0:T(8,128)(2,1)S(1)}, u32[]{:S(2)}, u32[]{:S(2)}) collective-permute-start(bf16[96,2048]{1,0:T(8,128)(2,1)S(1)} %after.1), channel_id=1, source_target_pairs={{0,480},{1,481},{2,482},{3,483},{4,484},{5,485},{6,486},{7,487},{8... | collective-permute-start | bytes 1179656 | tf_op jit(solution)/shard_map/ppermute | solution.py:230
  24.2 6.2 %pair_tile.3 = (f32[32,2048]{1,0:T(8,128)S(1)}, f32[32,2048]{1,0:T(8,128)S(1)}) custom-call(bf16[2048,256]{1,0:T(8,128)(2,1)S(1)} %get-tuple-element.11.refs_0_.left_ref, bf16[96,2048]{1,0:T(8,128)(2,1)S(1)} %pad_maximum_fusion.own_ref.refs_1_, bf16[96,2048]{1,0:T(8,128)(2,1)S(1)} %collective-permute-done.first_ref.refs_2_.refs_0_, ...), custom_call_target="tpu_custom_call" | custom-call | flops 1000 | bytes 1000 | tf_op jit(solution)/shard_map/pair_tile/pallas_call | solution.py:124
  30.5 0.0 collective-permute-done.1.refs_1_.refs_2_
  30.5 7.0 %pair_tile.4 = (bf16[32,2048]{1,0:T(8,128)(2,1)S(1)}, f32[32,2048]{1,0:T(8,128)S(1)}) custom-call(bf16[96,2048]{1,0:T(8,128)(2,1)S(1)} %collective-permute-done.first_ref.refs_2_.refs_0_, bf16[96,2048]{1,0:T(8,128)(2,1)S(1)} %collective-permute-done.1.refs_1_.refs_2_, f32[32,2048]{1,0:T(8,128)S(1)} %get-tuple-element.15.refs_2_), custom_call_target="tpu_custom_call" | custom-call | flops 1000 | bytes 1000 | tf_op jit(solution)/shard_map/pair_tile/pallas_call | solution.py:124
  37.5 11.4 %collective-permute-start.2 = (bf16[32,2048]{1,0:T(8,128)(2,1)S(1)}, bf16[32,2048]{1,0:T(8,128)(2,1)S(1)}, u32[]{:S(2)}, u32[]{:S(2)}) collective-permute-start(bf16[32,2048]{1,0:T(8,128)(2,1)S(1)} %get-tuple-element.18), channel_id=1, source_target_pairs={{0,511},{1,0},{2,1},{3,2},{4,3},{5,4},{6,5},{7,6},{8,7},{9,8},{10,... | collective-permute-start | bytes 393224 | tf_op jit(solution)/shard_map/ppermute | solution.py:230
  48.9 6.3 %pair_tile.5 = (f32[32,2048]{1,0:T(8,128)S(1)}, bf16[32,2048]{1,0:T(8,128)(2,1)S(1)}) custom-call(bf16[2048,256]{1,0:T(8,128)(2,1)S(1)} %get-tuple-element.11.refs_0_.left_ref, bf16[96,2048]{1,0:T(8,128)(2,1)S(1)} %pad_maximum_fusion.own_ref.refs_1_, bf16[96,2048]{1,0:T(8,128)(2,1)S(1)} %collective-permute-done.1.refs_1_.refs_2_, ...), custom_call_target="tpu_custom_call" | custom-call | flops 1000 | bytes 1000 | tf_op jit(solution)/shard_map/pair_tile/pallas_call | solution.py:124
  55.1 1.9 %collective-permute-start.3 = (bf16[32,2048]{1,0:T(8,128)(2,1)S(1)}, bf16[32,2048]{1,0:T(8,128)(2,1)S(1)}, u32[]{:S(2)}, u32[]{:S(2)}) collective-permute-start(bf16[32,2048]{1,0:T(8,128)(2,1)S(1)} %get-tuple-element.19), channel_id=1, source_target_pairs={{0,32},{1,33},{2,34},{3,35},{4,36},{5,37},{6,38},{7,39},{8,40},{9,... | collective-permute-start | bytes 393224 | tf_op jit(solution)/shard_map/ppermute | solution.py:230
  57.7 0.0 collective-permute-done.2.more_ref
  57.7 0.0 copy-start
  57.8 1.8 %last_self.1 = f32[32,2048]{1,0:T(8,128)S(1)} custom-call(bf16[2048,256]{1,0:T(8,128)(2,1)S(1)} %get-tuple-element.11.refs_0_.left_ref, bf16[96,2048]{1,0:T(8,128)(2,1)S(1)} %pad_maximum_fusion.own_ref.refs_1_, f32[32,2048]{1,0:T(8,128)S(1)} %get-tuple-element.17.acc_ref, bf16[32,2048]{1,0:T(8,128)(2,1)S(1)} %collective-permute-done.2.more_ref), custom_call_target="tpu_custom_call" | custom-call | flops 1000 | bytes 1000 | tf_op jit(solution)/shard_map/last_self/pallas_call | solution.py:200
  59.5 4.7 %collective-permute-done.3 = bf16[32,2048]{1,0:T(8,128)(2,1)S(1)} collective-permute-done((bf16[32,2048]{1,0:T(8,128)(2,1)S(1)}, bf16[32,2048]{1,0:T(8,128)(2,1)S(1)}, u32[]{:S(2)}, u32[]{:S(2)}) %collective-permute-start.3) | collective-permute-done | bytes 131104 | tf_op jit(solution)/shard_map/ppermute | solution.py:230
  64.3 0.0 copy-done
  64.3 0.2 multiply_reduce_fusion.1
  64.5 0.1 pad_maximum_fusion.1
  64.6 14.4 %all_to_all.12 = f32[32,1,64]{2,1,0:T(1,128)S(1)} all-to-all(f32[32,1,64]{2,1,0:T(1,128)S(1)} %broadcast_in_dim.4), channel_id=1, replica_groups=mesh['grp'=16,'dev'=32] {'dev'}, dimensions={0} | all-to-all | bytes 16384 | tf_op jit(solution)/shard_map/all_to_all | solution.py:237
  79.0 12.1 %all_to_all.13 = f32[16,1,64]{2,1,0:T(1,128)S(1)} all-to-all(f32[16,1,64]{2,1,0:T(1,128)S(1)} %broadcast_in_dim.5), channel_id=1, replica_groups=mesh['grp'=16,'dev'=32] {'grp'}, dimensions={0} | all-to-all | bytes 8192 | tf_op jit(solution)/shard_map/all_to_all | solution.py:237
  91.2 0.5 fusion.1
  91.7 0.8 multiply_bitcast_fusion
  (7 shorter events, 0.1 us)
Async XLA Ops:
  0.6 1.0 %copy-start.1 = (bf16[2048,64]{0,1:T(8,128)(2,1)S(1)}, bf16[2048,64]{0,1:T(8,128)(2,1)}, u32[]{:S(2)}) copy-start(bf16[2048,64]{0,1:T(8,128)(2,1)} %param.4) | copy-start | bytes 786436
  0.6 1.0 %copy-start.2 = (f32[64]{0:T(128)S(1)}, f32[64]{0:T(128)}, u32[]{:S(2)}) copy-start(f32[64]{0:T(128)} %param.5) | copy-start | bytes 772
  1.8 11.9 %collective-permute-start = (bf16[96,2048]{1,0:T(8,128)(2,1)S(1)}, bf16[96,2048]{1,0:T(8,128)(2,1)S(1)}, u32[]{:S(2)}, u32[]{:S(2)}) collective-permute-start(bf16[96,2048]{1,0:T(8,128)(2,1)S(1)} %pad_maximum_fusion.own_ref.refs_1_), channel_id=1, source_target_pairs={{0,1},{1,2},{2,3},{3,4},{4,5},{5,6},{6,7},{7,8},{8,9},{9,10},{10,1... | collective-permute-start | bytes 1179656 | tf_op jit(solution)/shard_map/ppermute | solution.py:230
  13.8 16.6 %collective-permute-start.1 = (bf16[96,2048]{1,0:T(8,128)(2,1)S(1)}, bf16[96,2048]{1,0:T(8,128)(2,1)S(1)}, u32[]{:S(2)}, u32[]{:S(2)}) collective-permute-start(bf16[96,2048]{1,0:T(8,128)(2,1)S(1)} %after.1), channel_id=1, source_target_pairs={{0,480},{1,481},{2,482},{3,483},{4,484},{5,485},{6,486},{7,487},{8... | collective-permute-start | bytes 1179656 | tf_op jit(solution)/shard_map/ppermute | solution.py:230
  37.5 20.3 %collective-permute-start.2 = (bf16[32,2048]{1,0:T(8,128)(2,1)S(1)}, bf16[32,2048]{1,0:T(8,128)(2,1)S(1)}, u32[]{:S(2)}, u32[]{:S(2)}) collective-permute-start(bf16[32,2048]{1,0:T(8,128)(2,1)S(1)} %get-tuple-element.18), channel_id=1, source_target_pairs={{0,511},{1,0},{2,1},{3,2},{4,3},{5,4},{6,5},{7,6},{8,7},{9,8},{10,... | collective-permute-start | bytes 393224 | tf_op jit(solution)/shard_map/ppermute | solution.py:230
  55.1 9.1 %collective-permute-start.3 = (bf16[32,2048]{1,0:T(8,128)(2,1)S(1)}, bf16[32,2048]{1,0:T(8,128)(2,1)S(1)}, u32[]{:S(2)}, u32[]{:S(2)}) collective-permute-start(bf16[32,2048]{1,0:T(8,128)(2,1)S(1)} %get-tuple-element.19), channel_id=1, source_target_pairs={{0,32},{1,33},{2,34},{3,35},{4,36},{5,37},{6,38},{7,39},{8,40},{9,... | collective-permute-start | bytes 393224 | tf_op jit(solution)/shard_map/ppermute | solution.py:230
  57.7 6.5 %copy-start = (f32[2048,32]{0,1:T(8,128)S(1)}, f32[2048,32]{0,1:T(8,128)}, u32[]{:S(2)}) copy-start(f32[2048,32]{0,1:T(8,128)} %param.6) | copy-start | bytes 786436

commit v5 on v4

--- a/solution.py
+++ b/solution.py
@@ -81,9 +81,9 @@
     ref = dict(zip(names, refs))
     rows_ref, cols_ref, right, out, back = (ref[name] for name in ("rows", "cols", "right", "out", "back"))
     count = rows_ref.shape[1]
-    left = ref["made"] if "made" in ref else ref["left"]
-    if "made" in ref:
-        left[...] = left_side(rows_ref[:feats, :])
+    left = ref["left"]
+    if "next_left" in ref:
+        ref["next_left"][...] = left_side(cols_ref[:feats, :])
     put_right(right, cols_ref[:feats, :])
     out[...] = ref["acc"][...]
     back[...] = ref["back_acc"][...] if "back_acc" in ref else jnp.zeros_like(back)
@@ -112,23 +112,28 @@
     ]
 
 
-def pair(rows, cols, acc, feats, left=None, back_acc=None, out_dtype=jnp.float32, back_dtype=jnp.float32):
+def pair(left, rows, cols, acc, feats, back_acc=None, out_dtype=jnp.float32, back_dtype=jnp.float32, next_left=False):
     probes, count = acc.shape
-    given = {"left": left, "rows": rows, "cols": cols, "acc": acc, "back_acc": back_acc}
-    given = {name: value for name, value in given.items() if value is not None}
-    made = {"right": pltpu.VMEM((DEPTH, count), jnp.bfloat16)}
-    if left is None:
-        made["made"] = pltpu.VMEM((count, DEPTH), jnp.bfloat16)
-    made["out"] = made["back"] = pltpu.VMEM((probes, count), jnp.float32)
-    names = [*given, "out_ref", "back_ref", *made, "dist0", "dist1", "tile0", "tile1"]
+    given = {"left": left, "rows": rows, "cols": cols, "acc": acc}
+    if back_acc is not None:
+        given["back_acc"] = back_acc
+    results = {
+        "out_ref": jax.ShapeDtypeStruct((probes, count), out_dtype),
+        "back_ref": jax.ShapeDtypeStruct((probes, count), back_dtype),
+    }
+    if next_left:
+        results["next_left"] = jax.ShapeDtypeStruct(left.shape, left.dtype)
+    made = {
+        "right": pltpu.VMEM((DEPTH, count), jnp.bfloat16),
+        "out": pltpu.VMEM((probes, count), jnp.float32),
+        "back": pltpu.VMEM((probes, count), jnp.float32),
+    }
+    names = [*given, *results, *made, "dist0", "dist1", "tile0", "tile1"]
     return pl.pallas_call(
         functools.partial(pair_kernel, feats, names),
-        out_shape=(
-            jax.ShapeDtypeStruct((probes, count), out_dtype),
-            jax.ShapeDtypeStruct((probes, count), back_dtype),
-        ),
+        out_shape=tuple(results.values()),
         in_specs=[VMEM] * len(given),
-        out_specs=[VMEM] * 2,
+        out_specs=(VMEM,) * len(results),
         scratch_shapes=[*made.values(), *stage_buffers()],
         compiler_params=PARAMS,
         cost_estimate=COST,
@@ -162,15 +167,15 @@
     run_steps(self_steps(cols), measure, apply, dists, tiles)
 
 
-def first_kernel(cols, feats, own_ref, left_ref, out_ref, copy_ref, right, dist0, dist1, tile0, tile1):
+def first_kernel(cols, feats, noise_ref, wide_ref, own_ref, left_ref, out_ref, copy_ref, right, dist0, dist1, tile0, tile1):
     left_ref[...] = left_side(own_ref[:feats, :])
     put_right(right, own_ref[:feats, :])
-    out_ref[...] = jnp.zeros_like(out_ref)
+    out_ref[...] = wide_ref[...] * (noise_ref[0] * (1.0 / 3.0))
     copy_ref[...] = own_ref[...]
     run_self(cols, feats, left_ref, own_ref, out_ref, right, (dist0, dist1), (tile0, tile1))
 
 
-def first_self(own, feats, cols):
+def first_self(noise, wide, own, feats, cols):
     count = own.shape[1]
     probes = own.shape[0] - feats
     return pl.pallas_call(
@@ -180,13 +185,13 @@
             jax.ShapeDtypeStruct((probes, count), jnp.float32),
             jax.ShapeDtypeStruct(own.shape, own.dtype),
         ),
-        in_specs=[VMEM],
+        in_specs=[pl.BlockSpec(memory_space=pltpu.SMEM), VMEM, VMEM],
         out_specs=[VMEM] * 3,
         scratch_shapes=[pltpu.VMEM((DEPTH, count), jnp.bfloat16), *stage_buffers()],
         compiler_params=PARAMS,
         cost_estimate=COST,
         name="first_self",
-    )(own)
+    )(noise, wide, own)
 
 
 def last_kernel(cols, feats, left_ref, own_ref, acc_ref, more_ref, out_ref, right, dist0, dist1, tile0, tile1):
@@ -230,12 +235,33 @@
     return lax.ppermute(shard, ("grp", "dev"), [(i, (i + by) % count) for i in range(count)])
 
 
-def total(partial):
-    for axis in ("dev", "grp"):
-        size = lax.axis_size(axis)
-        copies = jnp.broadcast_to(partial[None, :], (size, partial.shape[0]))
-        partial = jnp.sum(lax.all_to_all(copies, axis, 0, 0), axis=0)
-    return partial
+def gather(partial, axis):
+    size = lax.axis_size(axis)
+    return lax.all_to_all(jnp.broadcast_to(partial[None, :], (size, partial.shape[0])), axis, 0, 0)
+
+
+def finish_kernel(count, parts_ref, product_ref, out_ref, curvature_ref):
+    probes = product_ref.shape[0]
+    mean = jnp.sum(parts_ref[...], axis=0, keepdims=True) * (1.0 / count)
+    curvature_ref[...] = mean[:, :probes]
+    scale = lax.rsqrt(mean[:, probes:] + 1e-06)
+    row = lax.broadcasted_iota(jnp.int32, (probes, probes), 0)
+    col = lax.broadcasted_iota(jnp.int32, (probes, probes), 1)
+    scale = jnp.sum(jnp.where(row == col, scale, 0.0), axis=1, keepdims=True)
+    out_ref[...] = product_ref[...] * scale
+
+
+def finish(parts, product, count):
+    return pl.pallas_call(
+        functools.partial(finish_kernel, count),
+        out_shape=(
+            jax.ShapeDtypeStruct(product.shape, jnp.float32),
+            jax.ShapeDtypeStruct((1, product.shape[0]), jnp.float32),
+        ),
+        compiler_params=PARAMS,
+        cost_estimate=COST,
+        name="finish",
+    )(parts, product)
 
 
 def per_device(points, inv_scale, probes, noise):
@@ -248,23 +274,22 @@
     near = move(own, 1)
     columns = list(range(0, points.shape[0], COLS))
     late = len(columns) // 4
-    left, acc, again = first_self(own, feats, columns[:-late])
+    left, acc, again = first_self(noise, wide, own, feats, columns[:-late])
     wide_far = move(after(near, again), -width)
-    acc, near_acc = pair(own, near, acc, feats, left=left)
-    to_near, far_acc = pair(near, wide_far, near_acc, feats, out_dtype=jnp.bfloat16)
+    acc, near_acc, near_left = pair(left, own, near, acc, feats, next_left=True)
+    to_near, far_acc = pair(near_left, near, wide_far, near_acc, feats, out_dtype=jnp.bfloat16)
     from_near = move(to_near, -1)
-    acc, to_far = pair(own, wide_far, acc, feats, left=left, back_acc=far_acc, back_dtype=jnp.bfloat16)
+    acc, to_far = pair(left, own, wide_far, acc, feats, back_acc=far_acc, back_dtype=jnp.bfloat16)
     from_far = move(to_far, width)
     acc = last_self(left, own, acc, from_near, feats, columns[-late:])
-    product = noise[0] * wide + (acc + from_far.astype(jnp.float32)) * 3.0
+    product = (acc + from_far.astype(jnp.float32)) * 3.0
     count = lax.axis_size("grp") * width * probes.shape[0]
-    sums = total(
-        jnp.concatenate([jnp.sum(rounded.astype(jnp.float32) * product, axis=1), jnp.sum(product * product, axis=1)])
+    sums = jnp.concatenate(
+        [jnp.sum(rounded.astype(jnp.float32) * product, axis=1), jnp.sum(product * product, axis=1)]
     )
-    mean = sums / count
-    curvature, mean_square = jnp.split(mean, 2)
-    normalized = product * lax.rsqrt(mean_square + 1e-06)[:, None]
-    return (normalized.T, curvature)
+    sums = jnp.sum(gather(sums, "dev"), axis=0)
+    normalized, curvature = finish(gather(sums, "grp"), product, count)
+    return (normalized.T, curvature[0])
 
 
 def solution(mesh):

time: 92.8 us -> 91.9 us (level)
  other arithmetic: 2.77 us -> 1.43 us
    pallas_call x3 -> x4, Pallas kernels: 19.5 us -> 20 us  [the longest x3 19.1 us: pair(): pl.pallas_call(functools.partial(pair_kernel, feats, names), out_shape=tu...]
where the time goes in v5:
time: 91.9 us; the launch traced here: 91.6 us
  starting transfers between devices  31 us (34%)
  blocking collectives  26.4 us (29%)
  Pallas kernels  24.1 us (26%)
  waiting for transfers between devices  7.15 us (8%)
  other arithmetic  1.43 us (2%)
  between operations  1.39 us (2%)
    ppermute x4, starting transfers between devices, move(): lax.ppermute(shard, ('grp', 'dev'), [(i, (i + by) % count) for i in range...  31 us
    all_to_all x2, blocking collectives, gather(): lax.all_to_all(jnp.broadcast_to(partial[None, :], (size, partial.shape[0]...  26.4 us
    pallas_call x3, Pallas kernels, pair(): pl.pallas_call(functools.partial(pair_kernel, feats, names), out_shape=tu...  19.1 us
    ppermute x4, waiting for transfers between devices, move(): lax.ppermute(shard, ('grp', 'dev'), [(i, (i + by) % count) for i in range...  7.15 us
    pallas_call x1, Pallas kernels, first_self(): pl.pallas_call(functools.partial(first_kernel, cols, feats), out_shape=(j...  2.34 us
  transfers between devices with their start and end apart: 4, of which 2 were waited for; matrix products, arithmetic and copies ran while one was open for 0% of the time, Pallas kernels for 18%

profile of v5, /device:TPU:1, one launch (start us, length us, event | category | flops | bytes accessed | tf_op | source)
XLA Modules:
  0.0 91.6 jit_solution(15682457269256272119)
XLA Ops:
  0.6 0.0 copy-start.2
  0.6 0.0 copy-start.1
  0.6 1.0 %bitcast_convert_fusion = bf16[32,2048]{1,0:T(8,128)(2,1)S(1)} fusion(f32[2048,32]{0,1:T(8,128)} %param.6), kind=kLoop, calls=%fused_computation.7 | loop fusion | flops 65536 | bytes 393216 | tf_op jit(solution)/shard_map/convert_element_type | solution.py:271
  1.7 0.0 copy-done.2
  1.7 0.0 copy-done.1
  1.7 0.1 fusion
  1.8 0.0 copy-start
  1.8 7.3 %collective-permute-start = (bf16[96,2048]{1,0:T(8,128)(2,1)S(1)}, bf16[96,2048]{1,0:T(8,128)(2,1)S(1)}, u32[]{:S(2)}, u32[]{:S(2)}) collective-permute-start(bf16[96,2048]{1,0:T(8,128)(2,1)S(1)} %pad_maximum_fusion.own_ref.refs_1_), channel_id=1, source_target_pairs={{0,1},{1,2},{2,3},{3,4},{4,5},{5,6},{6,7},{7,8},{8,9},{9,10},{10,1... | collective-permute-start | bytes 1179656 | tf_op jit(solution)/shard_map/ppermute | solution.py:235
  9.8 0.0 copy-done
  9.8 2.3 %first_self.1 = (bf16[2048,256]{1,0:T(8,128)(2,1)S(1)}, f32[32,2048]{1,0:T(8,128)S(1)}, bf16[96,2048]{1,0:T(8,128)(2,1)S(1)}) custom-call(f32[1]{0:T(128)S(6)} %copy.7.noise_ref, f32[32,2048]{1,0:T(8,128)S(1)} %bitcast.10, bf16[96,2048]{1,0:T(8,128)(2,1)S(1)} %pad_maximum_fusion.own_ref.refs_1_), custom_call_target="tpu_custom_call" | custom-call | flops 1000 | bytes 1000 | tf_op jit(solution)/shard_map/first_self/pallas_call | solution.py:181
  12.2 1.7 %collective-permute-done.first_ref.refs_2_.refs_1_ = bf16[96,2048]{1,0:T(8,128)(2,1)S(1)} collective-permute-done((bf16[96,2048]{1,0:T(8,128)(2,1)S(1)}, bf16[96,2048]{1,0:T(8,128)(2,1)S(1)}, u32[]{:S(2)}, u32[]{:S(2)}) %collective-permute-start) | collective-permute-done | bytes 393248 | tf_op jit(solution)/shard_map/ppermute | solution.py:235
  14.0 10.4 %collective-permute-start.1 = (bf16[96,2048]{1,0:T(8,128)(2,1)S(1)}, bf16[96,2048]{1,0:T(8,128)(2,1)S(1)}, u32[]{:S(2)}, u32[]{:S(2)}) collective-permute-start(bf16[96,2048]{1,0:T(8,128)(2,1)S(1)} %after.1), channel_id=1, source_target_pairs={{0,480},{1,481},{2,482},{3,483},{4,484},{5,485},{6,486},{7,487},{8... | collective-permute-start | bytes 1179656 | tf_op jit(solution)/shard_map/ppermute | solution.py:235
  24.4 6.4 %pair_tile.3 = (f32[32,2048]{1,0:T(8,128)S(1)}, f32[32,2048]{1,0:T(8,128)S(1)}, bf16[2048,256]{1,0:T(8,128)(2,1)S(1)}) custom-call(bf16[2048,256]{1,0:T(8,128)(2,1)S(1)} %get-tuple-element.14.refs_0_.left_ref, bf16[96,2048]{1,0:T(8,128)(2,1)S(1)} %pad_maximum_fusion.own_ref.refs_1_, bf16[96,2048]{1,0:T(8,128)(2,1)S(1)} %collective-permute-done.first_ref.refs_2_.refs_1_, ...), custom_call_target="tpu_custom_call" | custom-call | flops 1000 | bytes 1000 | tf_op jit(solution)/shard_map/pair_tile/pallas_call | solution.py:132
  30.7 0.0 collective-permute-done.1.refs_2_
  30.7 6.5 %pair_tile.4 = (bf16[32,2048]{1,0:T(8,128)(2,1)S(1)}, f32[32,2048]{1,0:T(8,128)S(1)}) custom-call(bf16[2048,256]{1,0:T(8,128)(2,1)S(1)} %get-tuple-element.18.refs_0_, bf16[96,2048]{1,0:T(8,128)(2,1)S(1)} %collective-permute-done.first_ref.refs_2_.refs_1_, bf16[96,2048]{1,0:T(8,128)(2,1)S(1)} %collective-permute-done.1.refs_2_, ...), custom_call_target="tpu_custom_call" | custom-call | flops 1000 | bytes 1000 | tf_op jit(solution)/shard_map/pair_tile/pallas_call | solution.py:132
  37.2 11.4 %collective-permute-start.2 = (bf16[32,2048]{1,0:T(8,128)(2,1)S(1)}, bf16[32,2048]{1,0:T(8,128)(2,1)S(1)}, u32[]{:S(2)}, u32[]{:S(2)}) collective-permute-start(bf16[32,2048]{1,0:T(8,128)(2,1)S(1)} %get-tuple-element.22), channel_id=1, source_target_pairs={{0,511},{1,0},{2,1},{3,2},{4,3},{5,4},{6,5},{7,6},{8,7},{9,8},{10,... | collective-permute-start | bytes 393224 | tf_op jit(solution)/shard_map/ppermute | solution.py:235
  48.6 6.3 %pair_tile.5 = (f32[32,2048]{1,0:T(8,128)S(1)}, bf16[32,2048]{1,0:T(8,128)(2,1)S(1)}) custom-call(bf16[2048,256]{1,0:T(8,128)(2,1)S(1)} %get-tuple-element.14.refs_0_.left_ref, bf16[96,2048]{1,0:T(8,128)(2,1)S(1)} %pad_maximum_fusion.own_ref.refs_1_, bf16[96,2048]{1,0:T(8,128)(2,1)S(1)} %collective-permute-done.1.refs_2_, ...), custom_call_target="tpu_custom_call" | custom-call | flops 1000 | bytes 1000 | tf_op jit(solution)/shard_map/pair_tile/pallas_call | solution.py:132
  54.9 1.9 %collective-permute-start.3 = (bf16[32,2048]{1,0:T(8,128)(2,1)S(1)}, bf16[32,2048]{1,0:T(8,128)(2,1)S(1)}, u32[]{:S(2)}, u32[]{:S(2)}) collective-permute-start(bf16[32,2048]{1,0:T(8,128)(2,1)S(1)} %get-tuple-element.23), channel_id=1, source_target_pairs={{0,32},{1,33},{2,34},{3,35},{4,36},{5,37},{6,38},{7,39},{8,40},{9,... | collective-permute-start | bytes 393224 | tf_op jit(solution)/shard_map/ppermute | solution.py:235
  56.8 0.0 collective-permute-done.2.more_ref
  56.8 1.8 %last_self.1 = f32[32,2048]{1,0:T(8,128)S(1)} custom-call(bf16[2048,256]{1,0:T(8,128)(2,1)S(1)} %get-tuple-element.14.refs_0_.left_ref, bf16[96,2048]{1,0:T(8,128)(2,1)S(1)} %pad_maximum_fusion.own_ref.refs_1_, f32[32,2048]{1,0:T(8,128)S(1)} %get-tuple-element.21.acc_ref, bf16[32,2048]{1,0:T(8,128)(2,1)S(1)} %collective-permute-done.2.more_ref), custom_call_target="tpu_custom_call" | custom-call | flops 1000 | bytes 1000 | tf_op jit(solution)/shard_map/last_self/pallas_call | solution.py:205
  58.6 5.4 %collective-permute-done.3 = bf16[32,2048]{1,0:T(8,128)(2,1)S(1)} collective-permute-done((bf16[32,2048]{1,0:T(8,128)(2,1)S(1)}, bf16[32,2048]{1,0:T(8,128)(2,1)S(1)}, u32[]{:S(2)}, u32[]{:S(2)}) %collective-permute-start.3) | collective-permute-done | bytes 131104 | tf_op jit(solution)/shard_map/ppermute | solution.py:235
  64.0 0.2 multiply_reduce_fusion.1
  64.2 0.1 pad_maximum_fusion.1
  64.3 14.4 %all_to_all.14 = f32[32,1,64]{2,1,0:T(1,128)S(1)} all-to-all(f32[32,1,64]{2,1,0:T(1,128)S(1)} %broadcast_in_dim.4), channel_id=1, replica_groups=mesh['grp'=16,'dev'=32] {'dev'}, dimensions={0} | all-to-all | bytes 16384 | tf_op jit(solution)/shard_map/all_to_all | solution.py:240
  78.7 12.0 %all_to_all.15 = f32[16,1,64]{2,1,0:T(1,128)S(1)} all-to-all(f32[16,1,64]{2,1,0:T(1,128)S(1)} %broadcast_in_dim.5), channel_id=1, replica_groups=mesh['grp'=16,'dev'=32] {'grp'}, dimensions={0} | all-to-all | bytes 8192 | tf_op jit(solution)/shard_map/all_to_all | solution.py:240
  90.7 0.9 finish.1
  (5 shorter events, 0.1 us)
Async XLA Ops:
  0.6 1.0 %copy-start.2 = (f32[64]{0:T(128)S(1)}, f32[64]{0:T(128)}, u32[]{:S(2)}) copy-start(f32[64]{0:T(128)} %param.5) | copy-start | bytes 772
  0.6 1.0 %copy-start.1 = (bf16[2048,64]{0,1:T(8,128)(2,1)S(1)}, bf16[2048,64]{0,1:T(8,128)(2,1)}, u32[]{:S(2)}) copy-start(bf16[2048,64]{0,1:T(8,128)(2,1)} %param.4) | copy-start | bytes 786436
  1.8 8.0 %copy-start = (f32[2048,32]{0,1:T(8,128)S(1)}, f32[2048,32]{0,1:T(8,128)}, u32[]{:S(2)}) copy-start(f32[2048,32]{0,1:T(8,128)} %param.6) | copy-start | bytes 786436
  1.8 12.1 %collective-permute-start = (bf16[96,2048]{1,0:T(8,128)(2,1)S(1)}, bf16[96,2048]{1,0:T(8,128)(2,1)S(1)}, u32[]{:S(2)}, u32[]{:S(2)}) collective-permute-start(bf16[96,2048]{1,0:T(8,128)(2,1)S(1)} %pad_maximum_fusion.own_ref.refs_1_), channel_id=1, source_target_pairs={{0,1},{1,2},{2,3},{3,4},{4,5},{5,6},{6,7},{7,8},{8,9},{9,10},{10,1... | collective-permute-start | bytes 1179656 | tf_op jit(solution)/shard_map/ppermute | solution.py:235
  14.0 16.8 %collective-permute-start.1 = (bf16[96,2048]{1,0:T(8,128)(2,1)S(1)}, bf16[96,2048]{1,0:T(8,128)(2,1)S(1)}, u32[]{:S(2)}, u32[]{:S(2)}) collective-permute-start(bf16[96,2048]{1,0:T(8,128)(2,1)S(1)} %after.1), channel_id=1, source_target_pairs={{0,480},{1,481},{2,482},{3,483},{4,484},{5,485},{6,486},{7,487},{8... | collective-permute-start | bytes 1179656 | tf_op jit(solution)/shard_map/ppermute | solution.py:235
  37.2 19.6 %collective-permute-start.2 = (bf16[32,2048]{1,0:T(8,128)(2,1)S(1)}, bf16[32,2048]{1,0:T(8,128)(2,1)S(1)}, u32[]{:S(2)}, u32[]{:S(2)}) collective-permute-start(bf16[32,2048]{1,0:T(8,128)(2,1)S(1)} %get-tuple-element.22), channel_id=1, source_target_pairs={{0,511},{1,0},{2,1},{3,2},{4,3},{5,4},{6,5},{7,6},{8,7},{9,8},{10,... | collective-permute-start | bytes 393224 | tf_op jit(solution)/shard_map/ppermute | solution.py:235
  54.9 9.1 %collective-permute-start.3 = (bf16[32,2048]{1,0:T(8,128)(2,1)S(1)}, bf16[32,2048]{1,0:T(8,128)(2,1)S(1)}, u32[]{:S(2)}, u32[]{:S(2)}) collective-permute-start(bf16[32,2048]{1,0:T(8,128)(2,1)S(1)} %get-tuple-element.23), channel_id=1, source_target_pairs={{0,32},{1,33},{2,34},{3,35},{4,36},{5,37},{6,38},{7,39},{8,40},{9,... | collective-permute-start | bytes 393224 | tf_op jit(solution)/shard_map/ppermute | solution.py:235

commit v6 on v5

--- a/solution.py
+++ b/solution.py
@@ -25,7 +25,7 @@
     third_sq = jnp.maximum(third_sq, 1e-30)
     third = third_sq * lax.rsqrt(third_sq)
     decay = jnp.exp2(third * (-3.0 * LOG2E))
-    return ((third_sq + third + 1.0 / 3.0) * decay).astype(jnp.bfloat16)
+    return ((third_sq + (third + 1.0 / 3.0)) * decay).astype(jnp.bfloat16)
 
 
 def split3(wide):
@@ -94,8 +94,8 @@
 
     def apply(step, tile):
         row, rows, col = step
+        back[:, col : col + COLS] += dot(rows_ref[feats:, row : row + rows], tile[...], ((1,), (0,)))
         out[:, row : row + rows] += dot(cols_ref[feats:, col : col + COLS], tile[...], ((1,), (1,)))
-        back[:, col : col + COLS] += dot(rows_ref[feats:, row : row + rows], tile[...], ((1,), (0,)))
 
     steps = [(row, ROWS, col) for col in range(0, count, COLS) for row in range(0, count, ROWS)]
     run_steps(steps, measure, apply, (ref["dist0"], ref["dist1"]), (ref["tile0"], ref["tile1"]))
@@ -159,10 +159,10 @@
 
     def apply(step, tile):
         row, rows, col = step
+        out_ref[:, col : col + COLS] += dot(own_ref[feats:, row : row + rows], tile[:rows, :], ((1,), (0,)))
         above = min(rows, col - row)
         if above:
             out_ref[:, row : row + above] += dot(own_ref[feats:, col : col + COLS], tile[:above, :], ((1,), (1,)))
-        out_ref[:, col : col + COLS] += dot(own_ref[feats:, row : row + rows], tile[:rows, :], ((1,), (0,)))
 
     run_steps(self_steps(cols), measure, apply, dists, tiles)
 
@@ -214,22 +214,6 @@
     )(left, own, acc, more)
 
 
-def after_kernel(first_ref, own_ref, copy_ref):
-    copy_ref[...] = own_ref[...]
-
-
-def after(first, own):
-    return pl.pallas_call(
-        after_kernel,
-        out_shape=jax.ShapeDtypeStruct(own.shape, own.dtype),
-        in_specs=[VMEM] * 2,
-        out_specs=VMEM,
-        compiler_params=PARAMS,
-        cost_estimate=COST,
-        name="after",
-    )(first, own)
-
-
 def move(shard, by):
     count = lax.axis_size("grp") * lax.axis_size("dev")
     return lax.ppermute(shard, ("grp", "dev"), [(i, (i + by) % count) for i in range(count)])
@@ -271,18 +255,18 @@
     rounded = wide.astype(jnp.bfloat16)
     own = jnp.concatenate([scaled, rounded], axis=0)
     width = lax.axis_size("dev")
-    near = move(own, 1)
+    wide_far = move(own, -width)
     columns = list(range(0, points.shape[0], COLS))
     late = len(columns) // 4
     left, acc, again = first_self(noise, wide, own, feats, columns[:-late])
-    wide_far = move(after(near, again), -width)
-    acc, near_acc, near_left = pair(left, own, near, acc, feats, next_left=True)
-    to_near, far_acc = pair(near_left, near, wide_far, near_acc, feats, out_dtype=jnp.bfloat16)
+    near = move(again, 1)
+    acc, far_acc, far_left = pair(left, own, wide_far, acc, feats, next_left=True)
+    to_far, near_acc = pair(far_left, wide_far, near, far_acc, feats, out_dtype=jnp.bfloat16)
+    from_far = move(to_far, width)
+    acc, to_near = pair(left, own, near, acc, feats, back_acc=near_acc, back_dtype=jnp.bfloat16)
     from_near = move(to_near, -1)
-    acc, to_far = pair(left, own, wide_far, acc, feats, back_acc=far_acc, back_dtype=jnp.bfloat16)
-    from_far = move(to_far, width)
-    acc = last_self(left, own, acc, from_near, feats, columns[-late:])
-    product = (acc + from_far.astype(jnp.float32)) * 3.0
+    acc = last_self(left, own, acc, from_far, feats, columns[-late:])
+    product = (acc + from_near.astype(jnp.float32)) * 3.0
     count = lax.axis_size("grp") * width * probes.shape[0]
     sums = jnp.concatenate(
         [jnp.sum(rounded.astype(jnp.float32) * product, axis=1), jnp.sum(product * product, axis=1)]

time: 91.9 us -> 89.4 us (0.973)
  blocking collectives: 26.4 us -> 32.4 us
  waiting for transfers between devices: 7.15 us -> 1.56 us
  starting transfers between devices: 31 us -> 28.9 us
    all_to_all x2, blocking collectives: 26.4 us -> 32.4 us  [gather(): lax.all_to_all(jnp.broadcast_to(partial[None, :], (size, partial.shape[0]...]
    ppermute x4, waiting for transfers between devices: 7.15 us -> 1.56 us  [move(): lax.ppermute(shard, ('grp', 'dev'), [(i, (i + by) % count) for i in range...]
    ppermute x4, starting transfers between devices: 31 us -> 28.9 us  [move(): lax.ppermute(shard, ('grp', 'dev'), [(i, (i + by) % count) for i in range...]
  transfers between devices with their start and end apart: 4 -> 4, of which waited for: 2 -> 1; matrix products, arithmetic and copies ran while one was open for 0% -> 0% of each run, Pallas kernels for 18% -> 18%
where the time goes in v6:
time: 89.4 us; the launch traced here: 89.1 us
  blocking collectives  32.4 us (36%)
  starting transfers between devices  28.9 us (32%)
  Pallas kernels  23.3 us (26%)
  waiting for transfers between devices  1.56 us (2%)
  other arithmetic  1.43 us (2%)
  between operations  1.41 us (2%)
    all_to_all x2, blocking collectives, gather(): lax.all_to_all(jnp.broadcast_to(partial[None, :], (size, partial.shape[0]...  32.4 us
    ppermute x4, starting transfers between devices, move(): lax.ppermute(shard, ('grp', 'dev'), [(i, (i + by) % count) for i in range...  28.9 us
    pallas_call x3, Pallas kernels, pair(): pl.pallas_call(functools.partial(pair_kernel, feats, names), out_shape=tu...  18.2 us
    pallas_call x1, Pallas kernels, first_self(): pl.pallas_call(functools.partial(first_kernel, cols, feats), out_shape=(j...  2.55 us
  transfers between devices with their start and end apart: 4, of which 1 were waited for; matrix products, arithmetic and copies ran while one was open for 0% of the time, Pallas kernels for 18%

profile of v6, /device:TPU:1, one launch (start us, length us, event | category | flops | bytes accessed | tf_op | source)
XLA Modules:
  0.0 89.1 jit_solution(382946147755214289)
XLA Ops:
  0.6 0.0 copy-start.2
  0.6 0.0 copy-start.1
  0.6 1.0 %bitcast_convert_fusion = bf16[32,2048]{1,0:T(8,128)(2,1)S(1)} fusion(f32[2048,32]{0,1:T(8,128)} %param.6), kind=kLoop, calls=%fused_computation.7 | loop fusion | flops 65536 | bytes 393216 | tf_op jit(solution)/shard_map/convert_element_type | solution.py:255
  1.7 0.0 copy-done.2
  1.7 0.0 copy-done.1
  1.7 0.1 fusion
  1.8 0.0 copy-start
  1.8 7.9 %collective-permute-start.1 = (bf16[96,2048]{1,0:T(8,128)(2,1)S(1)}, bf16[96,2048]{1,0:T(8,128)(2,1)S(1)}, u32[]{:S(2)}, u32[]{:S(2)}) collective-permute-start(bf16[96,2048]{1,0:T(8,128)(2,1)S(1)} %pad_maximum_fusion.own_ref.refs_1_), channel_id=1, source_target_pairs={{0,480},{1,481},{2,482},{3,483},{4,484},{5,485},{6,486},{7,487},{8... | collective-permute-start | bytes 1179656 | tf_op jit(solution)/shard_map/ppermute | solution.py:219
  10.4 0.0 copy-done
  10.4 2.5 %first_self.1 = (bf16[2048,256]{1,0:T(8,128)(2,1)S(1)}, f32[32,2048]{1,0:T(8,128)S(1)}, bf16[96,2048]{1,0:T(8,128)(2,1)S(1)}) custom-call(f32[1]{0:T(128)S(6)} %copy.7.noise_ref, f32[32,2048]{1,0:T(8,128)S(1)} %bitcast.10, bf16[96,2048]{1,0:T(8,128)(2,1)S(1)} %pad_maximum_fusion.own_ref.refs_1_), custom_call_target="tpu_custom_call" | custom-call | flops 1000 | bytes 1000 | tf_op jit(solution)/shard_map/first_self/pallas_call | solution.py:181
  12.9 6.8 %collective-permute-start = (bf16[96,2048]{1,0:T(8,128)(2,1)S(1)}, bf16[96,2048]{1,0:T(8,128)(2,1)S(1)}, u32[]{:S(2)}, u32[]{:S(2)}) collective-permute-start(bf16[96,2048]{1,0:T(8,128)(2,1)S(1)} %get-tuple-element.15), channel_id=1, source_target_pairs={{0,1},{1,2},{2,3},{3,4},{4,5},{5,6},{6,7},{7,8},{8,9},{9,10},{10,1... | collective-permute-start | bytes 1179656 | tf_op jit(solution)/shard_map/ppermute | solution.py:219
  19.8 0.0 collective-permute-done.1.refs_2_.refs_1_
  19.8 6.2 %pair_tile.3 = (f32[32,2048]{1,0:T(8,128)S(1)}, f32[32,2048]{1,0:T(8,128)S(1)}, bf16[2048,256]{1,0:T(8,128)(2,1)S(1)}) custom-call(bf16[2048,256]{1,0:T(8,128)(2,1)S(1)} %get-tuple-element.14.refs_0_.left_ref, bf16[96,2048]{1,0:T(8,128)(2,1)S(1)} %pad_maximum_fusion.own_ref.refs_1_, bf16[96,2048]{1,0:T(8,128)(2,1)S(1)} %collective-permute-done.1.refs_2_.refs_1_, ...), custom_call_target="tpu_custom_call" | custom-call | flops 1000 | bytes 1000 | tf_op jit(solution)/shard_map/pair_tile/pallas_call | solution.py:132
  26.0 1.5 %collective-permute-done.refs_2_ = bf16[96,2048]{1,0:T(8,128)(2,1)S(1)} collective-permute-done((bf16[96,2048]{1,0:T(8,128)(2,1)S(1)}, bf16[96,2048]{1,0:T(8,128)(2,1)S(1)}, u32[]{:S(2)}, u32[]{:S(2)}) %collective-permute-start) | collective-permute-done | bytes 393248 | tf_op jit(solution)/shard_map/ppermute | solution.py:219
  27.5 6.0 %pair_tile.4 = (bf16[32,2048]{1,0:T(8,128)(2,1)S(1)}, f32[32,2048]{1,0:T(8,128)S(1)}) custom-call(bf16[2048,256]{1,0:T(8,128)(2,1)S(1)} %get-tuple-element.18.refs_0_, bf16[96,2048]{1,0:T(8,128)(2,1)S(1)} %collective-permute-done.1.refs_2_.refs_1_, bf16[96,2048]{1,0:T(8,128)(2,1)S(1)} %collective-permute-done.refs_2_, f32[32,2048]{1,0:T(8,128)S(1)} %get-tuple-element.19.refs_3_), custom_call_target="tpu_custom_call" | custom-call | flops 1000 | bytes 1000 | tf_op jit(solution)/shard_map/pair_tile/pallas_call | solution.py:132
  33.5 2.1 %collective-permute-start.2 = (bf16[32,2048]{1,0:T(8,128)(2,1)S(1)}, bf16[32,2048]{1,0:T(8,128)(2,1)S(1)}, u32[]{:S(2)}, u32[]{:S(2)}) collective-permute-start(bf16[32,2048]{1,0:T(8,128)(2,1)S(1)} %get-tuple-element.22), channel_id=1, source_target_pairs={{0,32},{1,33},{2,34},{3,35},{4,36},{5,37},{6,38},{7,39},{8,40},{9,... | collective-permute-start | bytes 393224 | tf_op jit(solution)/shard_map/ppermute | solution.py:219
  35.7 6.0 %pair_tile.5 = (f32[32,2048]{1,0:T(8,128)S(1)}, bf16[32,2048]{1,0:T(8,128)(2,1)S(1)}) custom-call(bf16[2048,256]{1,0:T(8,128)(2,1)S(1)} %get-tuple-element.14.refs_0_.left_ref, bf16[96,2048]{1,0:T(8,128)(2,1)S(1)} %pad_maximum_fusion.own_ref.refs_1_, bf16[96,2048]{1,0:T(8,128)(2,1)S(1)} %collective-permute-done.refs_2_, ...), custom_call_target="tpu_custom_call" | custom-call | flops 1000 | bytes 1000 | tf_op jit(solution)/shard_map/pair_tile/pallas_call | solution.py:132
  41.7 12.1 %collective-permute-start.3 = (bf16[32,2048]{1,0:T(8,128)(2,1)S(1)}, bf16[32,2048]{1,0:T(8,128)(2,1)S(1)}, u32[]{:S(2)}, u32[]{:S(2)}) collective-permute-start(bf16[32,2048]{1,0:T(8,128)(2,1)S(1)} %get-tuple-element.23), channel_id=1, source_target_pairs={{0,511},{1,0},{2,1},{3,2},{4,3},{5,4},{6,5},{7,6},{8,7},{9,8},{10,... | collective-permute-start | bytes 393224 | tf_op jit(solution)/shard_map/ppermute | solution.py:219
  53.8 0.0 collective-permute-done.2.more_ref
  53.8 1.7 %last_self.1 = f32[32,2048]{1,0:T(8,128)S(1)} custom-call(bf16[2048,256]{1,0:T(8,128)(2,1)S(1)} %get-tuple-element.14.refs_0_.left_ref, bf16[96,2048]{1,0:T(8,128)(2,1)S(1)} %pad_maximum_fusion.own_ref.refs_1_, f32[32,2048]{1,0:T(8,128)S(1)} %get-tuple-element.21.acc_ref, bf16[32,2048]{1,0:T(8,128)(2,1)S(1)} %collective-permute-done.2.more_ref), custom_call_target="tpu_custom_call" | custom-call | flops 1000 | bytes 1000 | tf_op jit(solution)/shard_map/last_self/pallas_call | solution.py:205
  55.5 0.0 collective-permute-done.3
  55.5 0.2 multiply_reduce_fusion.1
  55.7 0.1 pad_maximum_fusion.1
  55.8 16.9 %all_to_all.14 = f32[32,1,64]{2,1,0:T(1,128)S(1)} all-to-all(f32[32,1,64]{2,1,0:T(1,128)S(1)} %broadcast_in_dim.4), channel_id=1, replica_groups=mesh['grp'=16,'dev'=32] {'dev'}, dimensions={0} | all-to-all | bytes 16384 | tf_op jit(solution)/shard_map/all_to_all | solution.py:224
  72.7 15.5 %all_to_all.15 = f32[16,1,64]{2,1,0:T(1,128)S(1)} all-to-all(f32[16,1,64]{2,1,0:T(1,128)S(1)} %broadcast_in_dim.5), channel_id=1, replica_groups=mesh['grp'=16,'dev'=32] {'grp'}, dimensions={0} | all-to-all | bytes 8192 | tf_op jit(solution)/shard_map/all_to_all | solution.py:224
  88.2 0.9 finish.1
  (4 shorter events, 0.1 us)
Async XLA Ops:
  0.6 1.0 %copy-start.2 = (f32[64]{0:T(128)S(1)}, f32[64]{0:T(128)}, u32[]{:S(2)}) copy-start(f32[64]{0:T(128)} %param.5) | copy-start | bytes 772
  0.6 1.0 %copy-start.1 = (bf16[2048,64]{0,1:T(8,128)(2,1)S(1)}, bf16[2048,64]{0,1:T(8,128)(2,1)}, u32[]{:S(2)}) copy-start(bf16[2048,64]{0,1:T(8,128)(2,1)} %param.4) | copy-start | bytes 786436
  1.8 8.6 %copy-start = (f32[2048,32]{0,1:T(8,128)S(1)}, f32[2048,32]{0,1:T(8,128)}, u32[]{:S(2)}) copy-start(f32[2048,32]{0,1:T(8,128)} %param.6) | copy-start | bytes 786436
  1.8 17.9 %collective-permute-start.1 = (bf16[96,2048]{1,0:T(8,128)(2,1)S(1)}, bf16[96,2048]{1,0:T(8,128)(2,1)S(1)}, u32[]{:S(2)}, u32[]{:S(2)}) collective-permute-start(bf16[96,2048]{1,0:T(8,128)(2,1)S(1)} %pad_maximum_fusion.own_ref.refs_1_), channel_id=1, source_target_pairs={{0,480},{1,481},{2,482},{3,483},{4,484},{5,485},{6,486},{7,487},{8... | collective-permute-start | bytes 1179656 | tf_op jit(solution)/shard_map/ppermute | solution.py:219
  12.9 14.6 %collective-permute-start = (bf16[96,2048]{1,0:T(8,128)(2,1)S(1)}, bf16[96,2048]{1,0:T(8,128)(2,1)S(1)}, u32[]{:S(2)}, u32[]{:S(2)}) collective-permute-start(bf16[96,2048]{1,0:T(8,128)(2,1)S(1)} %get-tuple-element.15), channel_id=1, source_target_pairs={{0,1},{1,2},{2,3},{3,4},{4,5},{5,6},{6,7},{7,8},{8,9},{9,10},{10,1... | collective-permute-start | bytes 1179656 | tf_op jit(solution)/shard_map/ppermute | solution.py:219
  33.5 20.2 %collective-permute-start.2 = (bf16[32,2048]{1,0:T(8,128)(2,1)S(1)}, bf16[32,2048]{1,0:T(8,128)(2,1)S(1)}, u32[]{:S(2)}, u32[]{:S(2)}) collective-permute-start(bf16[32,2048]{1,0:T(8,128)(2,1)S(1)} %get-tuple-element.22), channel_id=1, source_target_pairs={{0,32},{1,33},{2,34},{3,35},{4,36},{5,37},{6,38},{7,39},{8,40},{9,... | collective-permute-start | bytes 393224 | tf_op jit(solution)/shard_map/ppermute | solution.py:219
  41.7 13.8 %collective-permute-start.3 = (bf16[32,2048]{1,0:T(8,128)(2,1)S(1)}, bf16[32,2048]{1,0:T(8,128)(2,1)S(1)}, u32[]{:S(2)}, u32[]{:S(2)}) collective-permute-start(bf16[32,2048]{1,0:T(8,128)(2,1)S(1)} %get-tuple-element.23), channel_id=1, source_target_pairs={{0,511},{1,0},{2,1},{3,2},{4,3},{5,4},{6,5},{7,6},{8,7},{9,8},{10,... | collective-permute-start | bytes 393224 | tf_op jit(solution)/shard_map/ppermute | solution.py:219

commit v7 on v6

--- a/solution.py
+++ b/solution.py
@@ -257,7 +257,7 @@
     width = lax.axis_size("dev")
     wide_far = move(own, -width)
     columns = list(range(0, points.shape[0], COLS))
-    late = len(columns) // 4
+    late = len(columns) // 8
     left, acc, again = first_self(noise, wide, own, feats, columns[:-late])
     near = move(again, 1)
     acc, far_acc, far_left = pair(left, own, wide_far, acc, feats, next_left=True)

time: 89.4 us -> 89.4 us (level)
  no operation moved by 1% of the time
where the time goes in v7:
time: 89.4 us; the launch traced here: 89.1 us
  blocking collectives  33.2 us (37%)
  starting transfers between devices  28.2 us (32%)
  Pallas kernels  23.4 us (26%)
  waiting for transfers between devices  1.56 us (2%)
  other arithmetic  1.43 us (2%)
  between operations  1.41 us (2%)
    all_to_all x2, blocking collectives, gather(): lax.all_to_all(jnp.broadcast_to(partial[None, :], (size, partial.shape[0]...  33.2 us
    ppermute x4, starting transfers between devices, move(): lax.ppermute(shard, ('grp', 'dev'), [(i, (i + by) % count) for i in range...  28.2 us
    pallas_call x3, Pallas kernels, pair(): pl.pallas_call(functools.partial(pair_kernel, feats, names), out_shape=tu...  18.2 us
    pallas_call x1, Pallas kernels, first_self(): pl.pallas_call(functools.partial(first_kernel, cols, feats), out_shape=(j...  3.3 us
  transfers between devices with their start and end apart: 4, of which 1 were waited for; matrix products, arithmetic and copies ran while one was open for 0% of the time, Pallas kernels for 18%

profile of v7, /device:TPU:1, one launch (start us, length us, event | category | flops | bytes accessed | tf_op | source)
XLA Modules:
  0.0 89.1 jit_solution(14178941444822510621)
XLA Ops:
  0.6 0.0 copy-start.2
  0.6 0.0 copy-start.1
  0.6 1.0 %bitcast_convert_fusion = bf16[32,2048]{1,0:T(8,128)(2,1)S(1)} fusion(f32[2048,32]{0,1:T(8,128)} %param.6), kind=kLoop, calls=%fused_computation.7 | loop fusion | flops 65536 | bytes 393216 | tf_op jit(solution)/shard_map/convert_element_type | solution.py:255
  1.7 0.0 copy-done.2
  1.7 0.0 copy-done.1
  1.7 0.1 fusion
  1.8 0.0 copy-start
  1.8 7.9 %collective-permute-start.1 = (bf16[96,2048]{1,0:T(8,128)(2,1)S(1)}, bf16[96,2048]{1,0:T(8,128)(2,1)S(1)}, u32[]{:S(2)}, u32[]{:S(2)}) collective-permute-start(bf16[96,2048]{1,0:T(8,128)(2,1)S(1)} %pad_maximum_fusion.own_ref.refs_1_), channel_id=1, source_target_pairs={{0,480},{1,481},{2,482},{3,483},{4,484},{5,485},{6,486},{7,487},{8... | collective-permute-start | bytes 1179656 | tf_op jit(solution)/shard_map/ppermute | solution.py:219
  10.4 0.0 copy-done
  10.4 3.3 %first_self.1 = (bf16[2048,256]{1,0:T(8,128)(2,1)S(1)}, f32[32,2048]{1,0:T(8,128)S(1)}, bf16[96,2048]{1,0:T(8,128)(2,1)S(1)}) custom-call(f32[1]{0:T(128)S(6)} %copy.7.noise_ref, f32[32,2048]{1,0:T(8,128)S(1)} %bitcast.10, bf16[96,2048]{1,0:T(8,128)(2,1)S(1)} %pad_maximum_fusion.own_ref.refs_1_), custom_call_target="tpu_custom_call" | custom-call | flops 1000 | bytes 1000 | tf_op jit(solution)/shard_map/first_self/pallas_call | solution.py:181
  13.7 6.8 %collective-permute-start = (bf16[96,2048]{1,0:T(8,128)(2,1)S(1)}, bf16[96,2048]{1,0:T(8,128)(2,1)S(1)}, u32[]{:S(2)}, u32[]{:S(2)}) collective-permute-start(bf16[96,2048]{1,0:T(8,128)(2,1)S(1)} %get-tuple-element.15), channel_id=1, source_target_pairs={{0,1},{1,2},{2,3},{3,4},{4,5},{5,6},{6,7},{7,8},{8,9},{9,10},{10,1... | collective-permute-start | bytes 1179656 | tf_op jit(solution)/shard_map/ppermute | solution.py:219
  20.5 0.0 collective-permute-done.1.refs_2_.refs_1_
  20.5 6.2 %pair_tile.3 = (f32[32,2048]{1,0:T(8,128)S(1)}, f32[32,2048]{1,0:T(8,128)S(1)}, bf16[2048,256]{1,0:T(8,128)(2,1)S(1)}) custom-call(bf16[2048,256]{1,0:T(8,128)(2,1)S(1)} %get-tuple-element.14.refs_0_.left_ref, bf16[96,2048]{1,0:T(8,128)(2,1)S(1)} %pad_maximum_fusion.own_ref.refs_1_, bf16[96,2048]{1,0:T(8,128)(2,1)S(1)} %collective-permute-done.1.refs_2_.refs_1_, ...), custom_call_target="tpu_custom_call" | custom-call | flops 1000 | bytes 1000 | tf_op jit(solution)/shard_map/pair_tile/pallas_call | solution.py:132
  26.7 1.5 %collective-permute-done.refs_2_ = bf16[96,2048]{1,0:T(8,128)(2,1)S(1)} collective-permute-done((bf16[96,2048]{1,0:T(8,128)(2,1)S(1)}, bf16[96,2048]{1,0:T(8,128)(2,1)S(1)}, u32[]{:S(2)}, u32[]{:S(2)}) %collective-permute-start) | collective-permute-done | bytes 393248 | tf_op jit(solution)/shard_map/ppermute | solution.py:219
  28.3 6.0 %pair_tile.4 = (bf16[32,2048]{1,0:T(8,128)(2,1)S(1)}, f32[32,2048]{1,0:T(8,128)S(1)}) custom-call(bf16[2048,256]{1,0:T(8,128)(2,1)S(1)} %get-tuple-element.18.refs_0_, bf16[96,2048]{1,0:T(8,128)(2,1)S(1)} %collective-permute-done.1.refs_2_.refs_1_, bf16[96,2048]{1,0:T(8,128)(2,1)S(1)} %collective-permute-done.refs_2_, f32[32,2048]{1,0:T(8,128)S(1)} %get-tuple-element.19.refs_3_), custom_call_target="tpu_custom_call" | custom-call | flops 1000 | bytes 1000 | tf_op jit(solution)/shard_map/pair_tile/pallas_call | solution.py:132
  34.3 2.1 %collective-permute-start.2 = (bf16[32,2048]{1,0:T(8,128)(2,1)S(1)}, bf16[32,2048]{1,0:T(8,128)(2,1)S(1)}, u32[]{:S(2)}, u32[]{:S(2)}) collective-permute-start(bf16[32,2048]{1,0:T(8,128)(2,1)S(1)} %get-tuple-element.22), channel_id=1, source_target_pairs={{0,32},{1,33},{2,34},{3,35},{4,36},{5,37},{6,38},{7,39},{8,40},{9,... | collective-permute-start | bytes 393224 | tf_op jit(solution)/shard_map/ppermute | solution.py:219
  36.4 6.0 %pair_tile.5 = (f32[32,2048]{1,0:T(8,128)S(1)}, bf16[32,2048]{1,0:T(8,128)(2,1)S(1)}) custom-call(bf16[2048,256]{1,0:T(8,128)(2,1)S(1)} %get-tuple-element.14.refs_0_.left_ref, bf16[96,2048]{1,0:T(8,128)(2,1)S(1)} %pad_maximum_fusion.own_ref.refs_1_, bf16[96,2048]{1,0:T(8,128)(2,1)S(1)} %collective-permute-done.refs_2_, ...), custom_call_target="tpu_custom_call" | custom-call | flops 1000 | bytes 1000 | tf_op jit(solution)/shard_map/pair_tile/pallas_call | solution.py:132
  42.4 11.3 %collective-permute-start.3 = (bf16[32,2048]{1,0:T(8,128)(2,1)S(1)}, bf16[32,2048]{1,0:T(8,128)(2,1)S(1)}, u32[]{:S(2)}, u32[]{:S(2)}) collective-permute-start(bf16[32,2048]{1,0:T(8,128)(2,1)S(1)} %get-tuple-element.23), channel_id=1, source_target_pairs={{0,511},{1,0},{2,1},{3,2},{4,3},{5,4},{6,5},{7,6},{8,7},{9,8},{10,... | collective-permute-start | bytes 393224 | tf_op jit(solution)/shard_map/ppermute | solution.py:219
  53.8 0.0 collective-permute-done.2.more_ref
  53.8 1.0 %last_self.1 = f32[32,2048]{1,0:T(8,128)S(1)} custom-call(bf16[2048,256]{1,0:T(8,128)(2,1)S(1)} %get-tuple-element.14.refs_0_.left_ref, bf16[96,2048]{1,0:T(8,128)(2,1)S(1)} %pad_maximum_fusion.own_ref.refs_1_, f32[32,2048]{1,0:T(8,128)S(1)} %get-tuple-element.21.acc_ref, bf16[32,2048]{1,0:T(8,128)(2,1)S(1)} %collective-permute-done.2.more_ref), custom_call_target="tpu_custom_call" | custom-call | flops 1000 | bytes 1000 | tf_op jit(solution)/shard_map/last_self/pallas_call | solution.py:205
  54.7 0.0 collective-permute-done.3
  54.8 0.2 multiply_reduce_fusion.1
  54.9 0.1 pad_maximum_fusion.1
  55.0 17.6 %all_to_all.14 = f32[32,1,64]{2,1,0:T(1,128)S(1)} all-to-all(f32[32,1,64]{2,1,0:T(1,128)S(1)} %broadcast_in_dim.4), channel_id=1, replica_groups=mesh['grp'=16,'dev'=32] {'dev'}, dimensions={0} | all-to-all | bytes 16384 | tf_op jit(solution)/shard_map/all_to_all | solution.py:224
  72.7 15.5 %all_to_all.15 = f32[16,1,64]{2,1,0:T(1,128)S(1)} all-to-all(f32[16,1,64]{2,1,0:T(1,128)S(1)} %broadcast_in_dim.5), channel_id=1, replica_groups=mesh['grp'=16,'dev'=32] {'grp'}, dimensions={0} | all-to-all | bytes 8192 | tf_op jit(solution)/shard_map/all_to_all | solution.py:224
  88.2 0.9 finish.1
  (4 shorter events, 0.1 us)
Async XLA Ops:
  0.6 1.0 %copy-start.2 = (f32[64]{0:T(128)S(1)}, f32[64]{0:T(128)}, u32[]{:S(2)}) copy-start(f32[64]{0:T(128)} %param.5) | copy-start | bytes 772
  0.6 1.0 %copy-start.1 = (bf16[2048,64]{0,1:T(8,128)(2,1)S(1)}, bf16[2048,64]{0,1:T(8,128)(2,1)}, u32[]{:S(2)}) copy-start(bf16[2048,64]{0,1:T(8,128)(2,1)} %param.4) | copy-start | bytes 786436
  1.8 8.6 %copy-start = (f32[2048,32]{0,1:T(8,128)S(1)}, f32[2048,32]{0,1:T(8,128)}, u32[]{:S(2)}) copy-start(f32[2048,32]{0,1:T(8,128)} %param.6) | copy-start | bytes 786436
  1.8 18.7 %collective-permute-start.1 = (bf16[96,2048]{1,0:T(8,128)(2,1)S(1)}, bf16[96,2048]{1,0:T(8,128)(2,1)S(1)}, u32[]{:S(2)}, u32[]{:S(2)}) collective-permute-start(bf16[96,2048]{1,0:T(8,128)(2,1)S(1)} %pad_maximum_fusion.own_ref.refs_1_), channel_id=1, source_target_pairs={{0,480},{1,481},{2,482},{3,483},{4,484},{5,485},{6,486},{7,487},{8... | collective-permute-start | bytes 1179656 | tf_op jit(solution)/shard_map/ppermute | solution.py:219
  13.7 14.6 %collective-permute-start = (bf16[96,2048]{1,0:T(8,128)(2,1)S(1)}, bf16[96,2048]{1,0:T(8,128)(2,1)S(1)}, u32[]{:S(2)}, u32[]{:S(2)}) collective-permute-start(bf16[96,2048]{1,0:T(8,128)(2,1)S(1)} %get-tuple-element.15), channel_id=1, source_target_pairs={{0,1},{1,2},{2,3},{3,4},{4,5},{5,6},{6,7},{7,8},{8,9},{9,10},{10,1... | collective-permute-start | bytes 1179656 | tf_op jit(solution)/shard_map/ppermute | solution.py:219
  34.3 19.5 %collective-permute-start.2 = (bf16[32,2048]{1,0:T(8,128)(2,1)S(1)}, bf16[32,2048]{1,0:T(8,128)(2,1)S(1)}, u32[]{:S(2)}, u32[]{:S(2)}) collective-permute-start(bf16[32,2048]{1,0:T(8,128)(2,1)S(1)} %get-tuple-element.22), channel_id=1, source_target_pairs={{0,32},{1,33},{2,34},{3,35},{4,36},{5,37},{6,38},{7,39},{8,40},{9,... | collective-permute-start | bytes 393224 | tf_op jit(solution)/shard_map/ppermute | solution.py:219
  42.4 12.3 %collective-permute-start.3 = (bf16[32,2048]{1,0:T(8,128)(2,1)S(1)}, bf16[32,2048]{1,0:T(8,128)(2,1)S(1)}, u32[]{:S(2)}, u32[]{:S(2)}) collective-permute-start(bf16[32,2048]{1,0:T(8,128)(2,1)S(1)} %get-tuple-element.23), channel_id=1, source_target_pairs={{0,511},{1,0},{2,1},{3,2},{4,3},{5,4},{6,5},{7,6},{8,7},{9,8},{10,... | collective-permute-start | bytes 393224 | tf_op jit(solution)/shard_map/ppermute | solution.py:219
